TPU v7x, 128 devices: a whole 4x4x4 slice. The times are simulated.
128 devices in a mesh: frames: 64 (over z, y, x_lo, core), dp: 2 (over x_hi).
Axes of the slice: x: 4 (x_hi: 2, x_lo: 2; x = x_hi * 2 + x_lo), y: 4, z: 4, core: 2. Of those that a mesh axis runs over, the one named last changes fastest.
Arguments:
- shifted: bfloat16 [2, 256, 16, 16, 640], P('dp', 'frames'), may hold values from -6 to 6
- out_grad: bfloat16 [2, 256, 16, 16, 640], P('dp', 'frames'), may hold values from -6 to 6
- conv_weight: bfloat16 [640, 5760], P('frames'), may hold values from -0.078125 to 0.078125
- norm_gain: float32 [640], replicated, may hold values from 0.5 to 2
- norm_bias: float32 [640], replicated, may hold values from -4 to 4
- shift_fwd: int32 [80], replicated, may hold values from 0 to 639, as said below
- shift_bwd: int32 [80], replicated, may hold values from 0 to 639, as said below
Outputs:
- in_grad: bfloat16 [2, 256, 16, 16, 640], P('dp', 'frames')
- weight_grad: float32 [640, 5760], P('frames')
- gain_grad: float32 [640], replicated
- bias_grad: float32 [640], replicated
Inputs may be any that keep to these rules, and one draw needn't show every extreme that they name: `shift_fwd`: 80 distinct channel numbers, none of them in shift_bwd. `shift_bwd`: 80 distinct channel numbers, none of them in shift_fwd.
All inputs are finite; a program needn't handle non-finite values.
Results may differ from a plain program's by a relative error of at most 0.003.
Values may be sent and summed in bfloat16 or wider, within the bound.
A program may use at most 128 MiB of HBM per device.

v0:
```python
import jax
import jax.numpy as jnp
from jax import lax
from jax.sharding import PartitionSpec as P

GROUP_CH = 20


epsilon = 1e-05


def with_halo(x, sides, width):
    for axis, dim in sides:
        size, length = (lax.axis_size(axis), x.shape[dim])
        up = [(i, (i + 1) % size) for i in range(size - 1)]
        down = [(j, i) for i, j in up]
        last = lax.slice_in_dim(x, length - width, length, axis=dim)
        first = lax.slice_in_dim(x, 0, width, axis=dim)
        before = lax.ppermute(last, axis, up)
        after = lax.ppermute(first, axis, down)
        x = jnp.concatenate([before, x, after], axis=dim)
    return x


def pad_space(values):
    return jnp.pad(values, ((0, 0), (1, 1), (1, 1), (0, 0)))


def on_device(shifted, out_grad, conv_weight, norm_gain, norm_bias, shift_fwd, shift_bwd):
    frames_local = shifted[0]
    grad_local = out_grad[0]
    frame_count, row_count, col_count, channels = frames_local.shape
    groups = channels // GROUP_CH
    whole_weight = lax.all_gather(conv_weight, "frames", axis=0, tiled=True)
    values = frames_local.astype(jnp.float32).reshape(
        frame_count, row_count * col_count, groups, GROUP_CH
    )
    center = jnp.mean(values, axis=(1, 3), keepdims=True)
    spread = jnp.mean(jnp.square(values - center), axis=(1, 3), keepdims=True)
    inverse = lax.rsqrt(spread + epsilon)
    grouped_normed = (values - center) * inverse
    normed = grouped_normed.reshape(frame_count, row_count, col_count, channels)
    before = normed * norm_gain + norm_bias
    activation = jax.nn.silu(before).astype(jnp.bfloat16)
    act_padded = pad_space(activation)
    grad_padded = pad_space(grad_local)
    grad_rows = grad_local.reshape(-1, channels)
    act_grad = jnp.zeros((grad_rows.shape[0], channels), jnp.float32)
    for tap_index in range(9):
        row_off, col_off = divmod(tap_index, 3)
        grad_view = grad_padded[
            :, 2 - row_off : 2 - row_off + row_count, 2 - col_off : 2 - col_off + col_count, :
        ].reshape(-1, channels)
        act_grad = act_grad + jnp.dot(
            grad_view,
            whole_weight[:, tap_index * channels : (tap_index + 1) * channels],
            preferred_element_type=jnp.float32,
        )
    scale = float(
        lax.axis_size("dp") * lax.axis_size("frames") * frame_count * row_count * col_count
    ) ** (-0.5)
    parts = []
    for tap_index in range(9):
        row_off, col_off = divmod(tap_index, 3)
        act_view = act_padded[
            :, row_off : row_off + row_count, col_off : col_off + col_count, :
        ].reshape(-1, channels)
        parts.append(
            lax.dot_general(
                grad_rows, act_view, (((0,), (0,)), ((), ())), preferred_element_type=jnp.float32
            )
        )
    kernel_shard = lax.psum_scatter(
        jnp.concatenate(parts, axis=1), "frames", scatter_dimension=0, tiled=True
    )
    kernel_shard = lax.psum(kernel_shard, "dp")
    weight_grad = kernel_shard * scale
    sigmoid_val = jax.nn.sigmoid(before)
    pre_grad = act_grad.reshape(before.shape) * sigmoid_val * (1.0 + before * (1.0 - sigmoid_val))
    gain_part = jnp.sum(pre_grad * normed, axis=(0, 1, 2))
    bias_part = jnp.sum(pre_grad, axis=(0, 1, 2))
    gain_total, bias_total = lax.psum((gain_part, bias_part), ("frames", "dp"))
    norm_grad = (pre_grad * norm_gain).reshape(values.shape)
    first_mean = jnp.mean(norm_grad, axis=(1, 3), keepdims=True)
    second_mean = jnp.mean(norm_grad * grouped_normed, axis=(1, 3), keepdims=True)
    shifted_grad = (
        ((norm_grad - first_mean - grouped_normed * second_mean) * inverse)
        .reshape(frames_local.shape)
        .astype(jnp.bfloat16)
    )
    channel_ids = jnp.arange(channels, dtype=jnp.int32)
    forward_match = channel_ids[None, :] == shift_fwd[:, None]
    backward_match = channel_ids[None, :] == shift_bwd[:, None]
    forward_select = forward_match.astype(jnp.bfloat16)
    backward_select = backward_match.astype(jnp.bfloat16)
    forward_mask = jnp.any(forward_match, axis=0)
    backward_mask = jnp.any(backward_match, axis=0)
    plane = row_count * col_count
    first_frame = shifted_grad[0].reshape(plane, channels)
    last_frame = shifted_grad[frame_count - 1].reshape(plane, channels)
    contract_channels = (((1,), (1,)), ((), ()))
    rim_first = lax.dot_general(
        forward_select, first_frame, contract_channels, preferred_element_type=jnp.float32
    ).astype(jnp.bfloat16)
    rim_last = lax.dot_general(
        backward_select, last_frame, contract_channels, preferred_element_type=jnp.float32
    ).astype(jnp.bfloat16)
    extended = with_halo(jnp.stack([rim_first, rim_last]), (("frames", 0),), 1)
    contract_fold = (((0,), (0,)), ((), ()))
    from_prev = lax.dot_general(
        extended[0], backward_select, contract_fold, preferred_element_type=jnp.float32
    ).astype(jnp.bfloat16)
    from_next = lax.dot_general(
        extended[3], forward_select, contract_fold, preferred_element_type=jnp.float32
    ).astype(jnp.bfloat16)
    from_prev = from_prev.reshape(1, row_count, col_count, channels)
    from_next = from_next.reshape(1, row_count, col_count, channels)
    later = jnp.concatenate([shifted_grad[1:], from_next], axis=0)
    earlier = jnp.concatenate([from_prev, shifted_grad[:-1]], axis=0)
    in_grad = jnp.where(forward_mask, later, jnp.where(backward_mask, earlier, shifted_grad))
    return (in_grad[None], weight_grad, gain_total * scale, bias_total * scale)


def solution(mesh):
    in_specs = (
        P("dp", "frames", None, None, None),
        P("dp", "frames", None, None, None),
        P("frames", None),
        P(),
        P(),
        P(),
        P(),
    )
    out_specs = (P("dp", "frames", None, None, None), P("frames", None), P(), P())
    return jax.shard_map(
        on_device, mesh=mesh, in_specs=in_specs, out_specs=out_specs, check_vma=False
    )
```

profile of v0, /device:TPU:1, one launch (start us, length us, event | category | flops | bytes accessed | tf_op | source)
XLA Modules:
  0.0 923.6 jit_solution(15676079137542957894)
XLA Ops:
  8.0 21.9 %reshape.226 = f32[4,256,32,20]{3,2,1,0:T(8,128)} reshape(bf16[1,4,16,16,640]{4,3,2,1,0:T(8,128)(2,1)} %param.7) | data formatting | bytes 3932160 | tf_op jit(solution)/shard_map/convert_element_type | solution.py:35
  31.5 11.5 %copy.33 = f32[4,256,32,20]{1,0,3,2:T(4,128)} copy(f32[4,256,32,20]{3,2,1,0:T(8,128)} %reshape.226) | data formatting | bytes 5242880 | tf_op jit(solution)/shard_map/convert_element_type | solution.py:35
  43.2 8.8 pad_slice_fusion.8
  52.0 78.7 %all-gather.3.cloned.1.call-done = bf16[64,10,5760]{2,1,0:T(8,128)(2,1)} async-done(((bf16[1,10,5760]{2,1,0:T(8,128)(2,1)}), bf16[64,10,5760]{2,1,0:T(8,128)(2,1)}) %all-gather.3.cloned.1.call-update) | async-done | bytes 7372816 | tf_op jit(solution)/shard_map/all_gather | solution.py:34
  130.7 13.8 %reshape.229 = bf16[640,5760]{1,0:T(8,128)(2,1)} reshape(bf16[64,10,5760]{2,1,0:T(8,128)(2,1)} %all-gather.3.cloned.1.call-done) | data formatting | bytes 14745600
  144.6 3.0 fusion.4
  155.3 2.8 fusion.18
  158.1 2.8 fusion.16
  160.9 6.2 fusion.28
  167.1 3.3 copy.31
  170.3 4.2 reshape.215
  174.5 16.5 %fusion.29 = (f32[4,32]{0,1:T(8,128)S(1)}, f32[4,32]{0,1:T(8,128)S(1)}) fusion(f32[4,32]{0,1:T(8,128)S(1)} %copy.34, f32[4,256,32,20]{1,0,3,2:T(4,128)} %copy.33, f32[4,32]{0,1:T(8,128)S(1)} %copy.32, f32[4,256,32,20]{1,0,3,2:T(4,128)} %reshape.215, f32[32,20]{1,0:T(8,128)S(1)} %add.134, f32[32,20]{1,0:T(8,128)S(1)} %mul.201), kind=kLoop, calls=%fused_computation.88 | loop fusion | flops 10485504 | bytes 5250048 | tf_op jit(solution)/shard_map/reduce_sum | solution.py:84
  191.6 3.6 multiply_convert_fusion
  195.2 3.0 pad_slice_fusion
  207.9 2.4 bitcast_dynamic-update-slice_fusion.4
  212.7 2.5 bitcast_dynamic-update-slice_fusion.2
  224.9 3.4 collective-permute-start.1
  228.2 67.9 %all-reduce.3 = (f32[640]{0:T(1024)S(1)}, f32[640]{0:T(1024)S(1)}) all-reduce(f32[640]{0:T(1024)S(1)} %get-tuple-element.25, f32[640]{0:T(1024)S(1)} %get-tuple-element.24), channel_id=1, replica_groups=mesh['frames'=64,'dp'=2] {'frames','dp'}, use_global_device_ids=true, to_apply=%region_11.12 | all-reduce | flops 1280 | bytes 10240 | tf_op jit(solution)/shard_map/psum | solution.py:82
  300.3 516.5 %all-reduce.9.cloned.1.call-done = f32[640,5760]{0,1:T(8,128)} async-done(((f32[640,5760]{0,1:T(8,128)}), f32[640,5760]{0,1:T(8,128)}) %all-reduce.9.cloned.1.call-update) | async-done | bytes 14745616
  816.7 5.1 constant_dynamic-slice_fusion
  823.3 4.4 maximum_select_fusion
  827.7 82.4 %all-reduce.7.cloned.1.call-done = f32[10,5760]{0,1:T(8,128)} async-done(((f32[10,5760]{0,1:T(8,128)}), f32[10,5760]{0,1:T(8,128)}) %all-reduce.7.cloned.1.call-update) | async-done | bytes 230416 | tf_op jit(solution)/shard_map/psum | solution.py:76
  910.1 3.7 broadcast_multiply_fusion
  913.8 3.0 copy.37
  (88 shorter events, 37.4 us)
Async XLA Ops:
  7.2 123.5 %all-gather.3.cloned.1.call-start = ((), (), s32[]{:S(2)}) async-start(), calls=%async_computation.1 | async-start | bytes 11980800 | tf_op jit(solution)/shard_map/all_gather | solution.py:34
  7.9 22.0 %copy-start = (bf16[1,4,16,16,640]{4,3,2,1,0:T(8,128)(2,1)S(1)}, bf16[1,4,16,16,640]{4,3,2,1,0:T(8,128)(2,1)}, u32[]{:S(2)}) copy-start(bf16[1,4,16,16,640]{4,3,2,1,0:T(8,128)(2,1)} %param.7) | copy-start | bytes 3932164
  7.9 808.8 %all-reduce.9.cloned.1.call-start = ((), (), s32[]{:S(2)}) async-start(), calls=%async_computation.2 | async-start | bytes 29491200
  31.5 11.5 %copy-start.12 = (f32[640]{0:T(1024)S(1)}, f32[640]{0:T(1024)}, u32[]{:S(2)}) copy-start(f32[640]{0:T(1024)} %param.11) | copy-start | bytes 7684
  31.5 11.6 %copy-start.13 = (f32[640]{0:T(1024)S(1)}, f32[640]{0:T(1024)}, u32[]{:S(2)}) copy-start(f32[640]{0:T(1024)} %param.10) | copy-start | bytes 7684
  144.5 3.7 copy-start.1
  144.6 4.0 copy-start.11
  148.6 1.3 copy-start.10
  149.9 1.3 copy-start.4
  151.3 1.3 copy-start.9
  152.6 1.3 copy-start.8
  154.0 1.3 copy-start.7
  155.3 2.8 copy-start.6
  195.2 3.0 copy-start.5
  220.1 0.7 copy-start.16
  220.1 1.9 copy-start.14
  220.1 1.9 copy-start.15
  220.1 690.0 %all-reduce.7.cloned.1.call-start = ((), (), s32[]{:S(2)}) async-start(), calls=%async_computation | async-start | bytes 5898240 | tf_op jit(solution)/shard_map/psum | solution.py:76
  222.4 75.8 %collective-permute-start = (bf16[1,80,256]{2,1,0:T(8,128)(2,1)S(1)}, bf16[1,80,256]{2,1,0:T(8,128)(2,1)S(1)}, u32[]{:S(2)}, u32[]{:S(2)}) collective-permute-start(bf16[1,80,256]{2,1,0:T(8,128)(2,1)S(1)} %fusion.1), channel_id=1, source_target_pairs={{2,0},{4,2},{6,4},{8,6},{10,8},{12,10},{14,12},{16,14},{18,16},{20... | collective-permute-start | bytes 122888 | tf_op jit(solution)/shard_map/ppermute | solution.py:20
  224.9 74.4 %collective-permute-start.1 = (bf16[1,80,256]{2,1,0:T(8,128)(2,1)S(1)}, bf16[1,80,256]{2,1,0:T(8,128)(2,1)S(1)}, u32[]{:S(2)}, u32[]{:S(2)}) collective-permute-start(bf16[1,80,256]{2,1,0:T(8,128)(2,1)S(1)} %fusion.2), channel_id=1, source_target_pairs={{0,2},{2,4},{4,6},{6,8},{8,10},{10,12},{12,14},{14,16},{16,18},{18... | collective-permute-start | bytes 122888 | tf_op jit(solution)/shard_map/ppermute | solution.py:19
  821.8 1.2 copy-start.2
  821.8 1.5 copy-start.3
Sparse Core Ops, SparseCore 0:
  9.7 120.9 all-gather.2
  220.2 596.4 all-reduce.8
  822.0 88.0 all-reduce.6
where the time goes:
time: 929 us; the launch traced here: 924 us
  waiting for transfers between devices  678 us (73%)
  local copies, waits for them, and re-layouts  81.4 us (9%)
  blocking collectives  67.9 us (7%)
  matrix products  45.7 us (5%)
  other arithmetic  29.7 us (3%)
  between operations  15 us (2%)
    unnamed x4, waiting for transfers between devices  517 us
    psum x1, waiting for transfers between devices, on_device(): kernel_shard = lax.psum(kernel_shard, 'dp')  82.4 us
    all_gather x1, waiting for transfers between devices, on_device(): whole_weight = lax.all_gather(conv_weight, 'frames', axis=0, tiled=True)  78.7 us
    psum x1, blocking collectives, on_device(): gain_total, bias_total = lax.psum((gain_part, bias_part), ('frames', 'dp'))  67.9 us
    convert_element_type x2, local copies, waits for them, and re-layouts, on_device(): frames_local.astype(jnp.float32)  33.4 us
    unnamed x38, local copies, waits for them, and re-layouts  25.6 us
    dot_general x9, matrix products, on_device(): lax.dot_general(grad_rows, act_view, (((0,), (0,)), ((), ())), preferred_...  21.8 us
    dot_general x9, matrix products, on_device(): jnp.dot(grad_view, whole_weight[:, tap_index * channels:(tap_index + 1) *...  21.3 us
  transfers between devices with their start and end apart: 5, of which 3 were waited for; matrix products, arithmetic and copies ran while one was open for 6% of the time, Pallas kernels for 0%

commit v1 on v0

v1 whole, which is shorter than its diff:
```python
import jax
import jax.numpy as jnp
from jax import lax
from jax.experimental import pallas as pl
from jax.experimental.pallas import tpu as pltpu
from jax.sharding import PartitionSpec as P

f32, bf16 = jnp.float32, jnp.bfloat16
MESH = pl.DeviceIdType.MESH
EPS = 1e-05
CH, HALF, WIDE = 640, 320, 1024
HIGH = lax.Precision.HIGHEST


def dot(a, b):
    return jnp.dot(a, b, preferred_element_type=f32)


def dot_nt(a, b):
    return lax.dot_general(a, b, (((1,), (1,)), ((), ())), preferred_element_type=f32)


def rows16(v, n):
    return pl.ds(pl.multiple_of(v, 16), n)


def div20(i):
    return (i * 3277) >> 16


def kernel(
    scale,
    x_ref, g_hbm, w_ref, gain_ref, bias_ref, fwd_ref, bwd_ref,
    ig_ref, wg_ref, gb_ref,
    xs, xb, gp, gt, pm, ap, p1, w, y_acc, pre,
    cen, inv, s1, s2, m1, m2,
    s_buf, wgs, xr, z1s, z1r, z2s, z2r, yf, ys, yr, ds_, dr,
    sgp, igs, igr, hs, hr, selm, ar_s, ar_r, ar_c,
    loc_sem, ex_s, ex_r, p1_s, p1_r, zo_s, zo_r, zf_s, zf_r, cr_s, cr_r, yi_s, yi_r,
    x_s, x_r, z1_ss, z1_rs, z2_ss, z2_rs, y_ss, y_rs, d_ss, d_rs, h_ss, h_rs, a_ss, a_rs,
):
    f = lax.axis_index("frames")
    d = lax.axis_index("dp")
    c = f % 2
    xl = (f // 2) % 2
    y = (f // 4) % 4
    z = f // 16
    x = d * 2 + xl
    y0 = y % 2
    y1 = y // 2

    def dev(zz, yy, xx, cc):
        return {"frames": ((zz * 4 + yy) * 2 + xx % 2) * 2 + cc, "dp": xx // 2}

    oc = 1 - c
    zp, zm, zo = (z + 1) % 4, (z + 3) % 4, (z + 2) % 4
    yin = y + 1 - 2 * y0
    ycross = (y + 3 + 2 * y0) % 4
    xin = x + 1 - 2 * xl
    xcross = (x + 3 + 2 * xl) % 4
    xop = (x + 2) % 4
    sib = dev(z, y, x, oc)
    nxt = {"frames": (f + 2) % 64, "dp": d}
    prv = {"frames": (f + 62) % 64, "dp": d}

    def remote(src, dst, ss, rs, to):
        return pltpu.make_async_remote_copy(
            src_ref=src, dst_ref=dst, send_sem=ss, recv_sem=rs, device_id=to, device_id_type=MESH
        )

    barrier = pltpu.get_barrier_semaphore()
    partners = [sib, nxt, prv]
    for yy, xx in ((yin, x), (y, xin), (yin, xin)):
        partners += [dev(z, yy, xx, 0), dev(z, yy, xx, 1)]
    for k in (2, 3):
        yy = (ycross, (y + 2) % 4)[k - 2]
        partners += [dev(z, yy, x, 0), dev(z, yy, x, 1)]
    partners += [dev(z, y, xcross, c), dev(z, y, xop, c)]
    partners += [dev(zp, y, x, c), dev(zm, y, x, c), dev(zo, y, x, c)]
    for to in partners:
        pl.semaphore_signal(barrier, inc=1, device_id=to, device_id_type=MESH)
    pl.semaphore_wait(barrier, len(partners))

    me8 = (y0 * 2 + xl) * 2 + c
    p1c = []
    k = 0
    for yy, xx, dc in ((y, x, 1), (y, xin, 0), (y, xin, 1), (yin, x, 0), (yin, x, 1), (yin, xin, 0), (yin, xin, 1)):
        cc = c + dc - 2 * c * dc
        p1c.append(remote(w_ref.at[cc], p1.at[me8], p1_s.at[k], p1_r.at[k], dev(z, yy, xx, cc)))
        k += 1
    for cp in p1c:
        cp.start()
    interior = (pl.ds(c * 4, 4), pl.ds(16, 256))
    g_local = pltpu.make_async_copy(g_hbm, gp.at[interior], loc_sem.at[0])
    g_remote = remote(g_hbm, gp.at[interior], ex_s.at[0], ex_r.at[0], sib)
    g_local.start()
    p1[me8] = w_ref[c]

    def split(t, _):
        r = rows16(t * 256, 256)
        v = x_ref[r, :].astype(f32)
        xs[0, r, :] = v[:, :HALF].astype(bf16)
        xs[1, r, :] = v[:, HALF:].astype(bf16)
        return 0

    lax.fori_loop(0, 4, split, 0)
    x_remote = remote(xs.at[oc], xb, ex_s.at[1], ex_r.at[1], sib)
    x_remote.start()
    g_remote.start()

    def read_x(t):
        r = rows16((t % 4) * 256, 256)
        mine = xs[c, r, :]
        other = xb[r, :]
        return jnp.where(t // 4 == c, mine, other).astype(f32)

    zero16 = jnp.zeros((16, CH), bf16)
    zero16w = jnp.zeros((16, WIDE), bf16)
    for t in range(8):
        gp[t, 0:16, :] = zero16
        gp[t, 272:288, :] = zero16
        ap[t, 0:16, :] = zero16w
        ap[t, 272:288, :] = zero16w

    oi = lax.broadcasted_iota(jnp.int32, (CH, CH), 0)
    li = lax.broadcasted_iota(jnp.int32, (CH, CH), 1)
    q = (oi >= HALF).astype(jnp.int32)
    rr = oi - HALF * q
    zy = div20(rr)
    src_row = (2 * zy + (q + xl - 2 * q * xl)) * 20 + (rr - 20 * zy)
    pm[...] = (li == src_row).astype(f32).astype(bf16)
    gi = div20(lax.broadcasted_iota(jnp.int32, (HALF, HALF), 0))
    gj = div20(lax.broadcasted_iota(jnp.int32, (HALF, HALF), 1))
    group_mean = jnp.where(gi == gj, 1.0 / 5120.0, 0.0).astype(f32)

    def spread_groups(v):
        return jnp.dot(v, group_mean, preferred_element_type=f32, precision=HIGH)

    mine0 = c == 0
    gain = jnp.where(mine0, gain_ref[:, :HALF], gain_ref[:, HALF:])
    bias = jnp.where(mine0, bias_ref[:, :HALF], bias_ref[:, HALF:])

    def transpose(t):
        gt[:, pl.ds(pl.multiple_of(t * 256, 256), 256)] = dot_nt(pm[...], gp[t, 16:272, :]).astype(bf16)

    g_local.wait()

    def transpose_mine(i, _):
        transpose(c * 4 + i)
        return 0

    lax.fori_loop(0, 4, transpose_mine, 0)

    for cp in p1c:
        cp.wait_recv()
    blk = z * 2 + y1
    oblk = 1 - 2 * y1
    for lb in range(8):
        for a in range(3):
            r = (lb * 3 + a) * 10
            piece = jnp.concatenate([p1[s, r : r + 10, :].astype(f32) for s in range(8)], axis=0)
            w[a, blk, :, lb * 128 : lb * 128 + 128] = piece.astype(bf16)

    def lanes(qq, n=256):
        return pl.ds(pl.multiple_of(qq * 256, 256), n)

    def wsl(b, qq):
        return w.at[:, b, :, lanes(qq)]

    def z_own(k, qq):
        s = wsl(blk, qq)
        return remote(s, s, zo_s.at[k, qq], zo_r.at[k, qq], dev((zp, zm)[k], y, x, c))

    def z_fwd(qq):
        up = qq < 2
        s = wsl((zm if up else zp) * 2 + y1, qq)
        return remote(s, s, zf_s.at[qq], zf_r.at[qq], dev(zp if up else zm, y, x, c))

    zrel = (z, zm, zp, zo)

    def cross(k, h):
        s = wsl(zrel[k] * 2 + y1, 2 * h + 1 - y0)
        return remote(s, s, cr_s.at[k, h], cr_r.at[k, h], dev(z, ycross, x, c))

    def inner(k, h):
        s = wsl(zrel[k] * 2 + 1 - y1, 2 * h + y0)
        return remote(s, s, yi_s.at[k, h], yi_r.at[k, h], dev(z, yin, x, c))

    cross(0, 0).start()
    for qq in (0, 1):
        z_own(0, qq).start()
        z_own(1, qq).start()
    cross(0, 1).start()
    for qq in (2, 3):
        z_own(0, qq).start()
        z_own(1, qq).start()

    def hook_z(h):
        for qq in (2 * h, 2 * h + 1):
            z_own(0, qq).wait_recv()
            z_own(1, qq).wait_recv()
            z_fwd(qq).start()
        cross(1, h).start()
        cross(2, h).start()

    def hook_opp(h):
        z_fwd(2 * h).wait_recv()
        z_fwd(2 * h + 1).wait_recv()
        cross(3, h).start()

    def hook_in(k, h):
        cross(k, h).wait_recv()
        inner(k, h).start()

    x_remote.wait_recv()

    def stat_sum(t, _):
        s1[pl.ds(t, 1), :] = jnp.sum(read_x(t), axis=0, keepdims=True)
        return 0

    lax.fori_loop(0, 8, stat_sum, 0)
    cen[...] = spread_groups(s1[...])

    def stat_sq(t, _):
        v = read_x(t) - cen[pl.ds(t, 1), :]
        s2[pl.ds(t, 1), :] = jnp.sum(v * v, axis=0, keepdims=True)
        return 0

    lax.fori_loop(0, 8, stat_sq, 0)
    inv[...] = lax.rsqrt(spread_groups(s2[...]) + EPS)

    col = lax.broadcasted_iota(jnp.int32, (256, HALF), 0) % 16

    def normed_of(t):
        return (read_x(t) - cen[pl.ds(t, 1), :]) * inv[pl.ds(t, 1), :]

    def forward(t, _):
        before = normed_of(t) * gain + bias
        act = before / (1.0 + jnp.exp(-before))
        left = jnp.where(col == 0, 0.0, pltpu.roll(act, 1, 0))
        right = jnp.where(col == 15, 0.0, pltpu.roll(act, 255, 0))
        cat = jnp.concatenate([left, act, right, jnp.zeros((256, WIDE - 3 * HALF), f32)], axis=1)
        ap[t, 16:272, :] = cat.astype(bf16)
        return 0

    lax.fori_loop(0, 8, forward, 0)
    g_remote.wait_recv()

    def transpose_other(i, _):
        transpose(oc * 4 + i)
        return 0

    lax.fori_loop(0, 4, transpose_other, 0)
    hook_z(0)
    hook_in(0, 0)

    def x_copy(i):
        n = i % 2
        to = xin + n * (xcross - xin)
        return remote(wgs.at[i], xr.at[i], x_s.at[i], x_r.at[i], dev(z, y, to, c))

    def wg_step(i, _):
        a, n = i // 2, i % 2
        cols = pl.ds(pl.multiple_of(n * 512, 512), 512)
        acc = None
        for t in range(8):
            v = dot(gt[:, t * 256 : t * 256 + 256], ap[t, rows16(a * 16, 256), cols])
            acc = v if acc is None else acc + v
        s_buf[i] = acc[:HALF, :]
        wgs[i] = acc[HALF:, :].astype(bf16)
        x_copy(i).start()

        @pl.when(i == 0)
        def _():
            hook_in(0, 1)

        @pl.when(i == 1)
        def _():
            hook_z(1)
            hook_in(1, 0)

        @pl.when(i == 2)
        def _():
            hook_opp(0)
            hook_in(2, 0)

        @pl.when(i == 3)
        def _():
            hook_opp(1)

        @pl.when(i == 4)
        def _():
            hook_in(3, 0)

        @pl.when(i == 5)
        def _():
            hook_in(1, 1)

        return 0

    lax.fori_loop(0, 6, wg_step, 0)

    def z1_copy(i, k):
        return remote(z1s.at[i, k], z1r.at[i, k], z1_ss.at[i, k], z1_rs.at[i, k], dev((zp, zm)[k], y, x, c))

    def z2_copy(i, k):
        return remote(z2s.at[i, k], z2r.at[i, k], z2_ss.at[i, k], z2_rs.at[i, k], dev((zp, zm)[k], y, x, c))

    def y_copy(i, r):
        dy, dc = r // 2, r % 2
        yy, cc = (y + dy) % 4, c + dc - 2 * c * dc
        return remote(ys.at[i, yy * 2 + cc], yr.at[i, r], y_ss.at[i, r], y_rs.at[i, r], dev(z, yy, x, cc))

    def d_copy(i):
        return remote(ds_.at[i], dr.at[i], d_ss.at[i], d_rs.at[i], dev(z, y, xop, c))

    def block(b):
        return rows16(b * 80, 80)

    def stage1(i):
        x_copy(i).wait_recv()
        s_buf[i] = s_buf[i] + xr[i].astype(f32)
        z1s[i, 0] = s_buf[i, block(zo), 0:256].astype(bf16)
        z1s[i, 1] = s_buf[i, block(zo), 256:512].astype(bf16)
        z1_copy(i, 0).start()
        z1_copy(i, 1).start()

    def stage2(i):
        z1_copy(i, 0).wait_recv()
        z2s[i, 0, :, 0:256] = (s_buf[i, block(zp), 0:256] + z1r[i, 0].astype(f32)).astype(bf16)
        z2s[i, 0, :, 256:512] = s_buf[i, block(zp), 256:512].astype(bf16)
        z2_copy(i, 0).start()
        z1_copy(i, 1).wait_recv()
        z2s[i, 1, :, 0:256] = s_buf[i, block(zm), 0:256].astype(bf16)
        z2s[i, 1, :, 256:512] = (s_buf[i, block(zm), 256:512] + z1r[i, 1].astype(f32)).astype(bf16)
        z2_copy(i, 1).start()

    def stage3(i):
        z2_copy(i, 0).wait_recv()
        z2_copy(i, 1).wait_recv()
        total = s_buf[i, block(z), :] + z2r[i, 0].astype(f32) + z2r[i, 1].astype(f32)
        total = jnp.concatenate([total, jnp.zeros((8, 512), f32)], axis=0)
        for k in range(8):
            piece = total[10 * k : 10 * k + 16, :]
            yf[i, k] = piece
            ys[i, k] = piece.astype(bf16)
        for r in range(1, 8):
            y_copy(i, r).start()

    def stage4(i):
        for r in range(1, 8):
            y_copy(i, r).wait_recv()
        own = yf[i, y * 2 + c]
        for dy in (1, 2, 3):
            own = own + yr[i, 2 * dy].astype(f32)
        other = yr[i, 1].astype(f32)
        for dy in (1, 2, 3):
            other = other + yr[i, 2 * dy + 1].astype(f32)
        ds_[i, 0] = own
        ds_[i, 1] = other
        d_copy(i).start()

    def stage5(i):
        d_copy(i).wait_recv()
        own = (ds_[i, 0] + dr[i, 0]) * scale
        other = (ds_[i, 1] + dr[i, 1]) * scale
        a, n = i // 2, i % 2
        cols = pl.ds(pl.multiple_of(n * 512, 512), 512)
        wg_ref[0, a, :, cols] = jnp.where(mine0, own, other)
        wg_ref[1, a, :, cols] = jnp.where(mine0, other, own)

    stages = (stage1, stage2, stage3, stage4, stage5)

    def rs_slot(s):
        for k in range(5):
            i = s - k

            @pl.when(jnp.logical_and(i >= 0, i < 6))
            def _(k=k, i=i):
                stages[k](i)

    hook_in(2, 1)
    for k in range(4):
        inner(k, 0).wait_recv()

    def act_step(i, _):
        n, tt = i // 4, i % 4

        @pl.when(i == 0)
        def _():
            hook_in(3, 1)

        @pl.when(i == 4)
        def _():
            for k in range(4):
                inner(k, 1).wait_recv()

        cols = pl.ds(pl.multiple_of(n * 512, 512), 512)
        lhs = jnp.concatenate(
            [
                jnp.concatenate([gp[tt * 2 + t, 16 * (2 - a) : 16 * (2 - a) + 256, :] for a in range(3)], axis=1)
                for t in range(2)
            ],
            axis=0,
        )
        rhs = w[:, :, :, cols].reshape(3 * CH, 512)
        y_acc[rows16(tt * 512, 512), cols] = dot(lhs, rhs)
        rs_slot(i)
        return 0

    lax.fori_loop(0, 8, act_step, 0)

    def back1(t, _):
        r = rows16(t * 256, 256)
        v = y_acc[r, :]
        right = jnp.where(col == 15, 0.0, pltpu.roll(v[:, :HALF], 255, 0))
        left = jnp.where(col == 0, 0.0, pltpu.roll(v[:, 2 * HALF : 3 * HALF], 1, 0))
        act_grad = right + v[:, HALF : 2 * HALF] + left
        normed = normed_of(t)
        before = normed * gain + bias
        g = 1.0 / (1.0 + jnp.exp(-before))
        p = act_grad * g * (1.0 + before * (1.0 - g))
        pre[r, :] = p
        s1[pl.ds(t, 1), :] = jnp.sum(p * normed, axis=0, keepdims=True)
        s2[pl.ds(t, 1), :] = jnp.sum(p, axis=0, keepdims=True)
        return 0

    lax.fori_loop(0, 8, back1, 0)
    m1[...] = spread_groups(s2[...] * gain)
    m2[...] = spread_groups(s1[...] * gain)

    own_sum = jnp.concatenate(
        [jnp.sum(s1[...], axis=0, keepdims=True), jnp.sum(s2[...], axis=0, keepdims=True), jnp.zeros((6, HALF), f32)],
        axis=0,
    )

    def ar_copy(st, k):
        to = (
            (dev(z, y, xin, c), dev(z, y, xcross, c), dev(z, y, xop, c)),
            (dev(z, yin, x, c), dev(z, ycross, x, c), dev(z, (y + 2) % 4, x, c)),
            (dev(zp, y, x, c), dev(zm, y, x, c), dev(zo, y, x, c)),
        )[st][k]
        return remote(ar_s.at[st], ar_r.at[st, k], a_ss.at[st, k], a_rs.at[st, k], to)

    def ar_send(st, v):
        ar_s[st] = v
        for k in range(3):
            ar_copy(st, k).start()

    def ar_sum(st):
        v = ar_s[st]
        for k in range(3):
            ar_copy(st, k).wait_recv()
        return v + ar_r[st, 0] + ar_r[st, 1] + ar_r[st, 2]

    ar_send(0, own_sum)

    def back2(t, _):
        r = rows16(t * 256, 256)
        v = pre[r, :] * gain - m1[pl.ds(t, 1), :] - normed_of(t) * m2[pl.ds(t, 1), :]
        sgp[t + 1] = (v * inv[pl.ds(t, 1), :]).astype(bf16)
        return 0

    back2(0, 0)
    back2(7, 0)

    ch_id = lax.broadcasted_iota(jnp.int32, (HALF, 128), 0) + c * HALF
    selm[0] = (ch_id == bwd_ref[...]).astype(f32).astype(bf16)
    selm[1] = (ch_id == fwd_ref[...]).astype(f32).astype(bf16)
    hs[0] = dot(sgp[8], selm[0]).astype(bf16)
    hs[1] = dot(sgp[1], selm[1]).astype(bf16)
    halo = [
        remote(hs.at[0], hr.at[0], h_ss.at[0], h_rs.at[0], nxt),
        remote(hs.at[1], hr.at[1], h_ss.at[1], h_rs.at[1], prv),
    ]
    halo[0].start()
    halo[1].start()
    ones = jnp.ones((8, 128), bf16)
    bwd_mask = dot_nt(ones, selm[0])[0:1, :] > 0.5
    fwd_mask = dot_nt(ones, selm[1])[0:1, :] > 0.5

    rs_slot(8)
    lax.fori_loop(1, 7, back2, 0)
    ar_send(1, ar_sum(0))
    rs_slot(9)
    halo[0].wait_recv()
    halo[1].wait_recv()
    keep_prev = jnp.where(f >= 2, 1.0, 0.0)
    keep_next = jnp.where(f < 62, 1.0, 0.0)
    sgp[0] = (dot_nt(hr[0], selm[0]) * keep_prev).astype(bf16)
    sgp[9] = (dot_nt(hr[1], selm[1]) * keep_next).astype(bf16)

    def shift(t):
        v = jnp.where(bwd_mask, sgp[t].astype(f32), sgp[t + 1].astype(f32))
        return jnp.where(fwd_mask, sgp[t + 2].astype(f32), v)

    def shift_other(i, _):
        igs[i] = shift(oc * 4 + i).astype(bf16)
        return 0

    lax.fori_loop(0, 4, shift_other, 0)
    i_copy = remote(igs, igr, ex_s.at[2], ex_r.at[2], sib)
    i_copy.start()
    ar_send(2, ar_sum(1))
    rs_slot(10)
    total = ar_sum(2)
    ar_c[0] = total
    c_copy = remote(ar_c.at[0], ar_c.at[1], ex_s.at[3], ex_r.at[3], sib)
    c_copy.start()
    i_copy.wait_recv()

    def assemble(i, _):
        own = shift(c * 4 + i)
        other = igr[i].astype(f32)
        v = jnp.concatenate([jnp.where(mine0, own, other), jnp.where(mine0, other, own)], axis=1)
        ig_ref[rows16(i * 256, 256), :] = v.astype(bf16)
        return 0

    lax.fori_loop(0, 4, assemble, 0)
    c_copy.wait_recv()
    own = ar_c[0] * scale
    other = ar_c[1] * scale
    gb_ref[0] = jnp.where(mine0, own, other)
    gb_ref[1] = jnp.where(mine0, other, own)

    for cp in p1c:
        cp.wait_send()
    for cp in (g_remote, x_remote, i_copy, c_copy, halo[0], halo[1]):
        cp.wait_send()
    for qq in range(4):
        z_own(0, qq).wait_send()
        z_own(1, qq).wait_send()
        z_fwd(qq).wait_send()
    for k in range(4):
        for h in range(2):
            cross(k, h).wait_send()
            inner(k, h).wait_send()
    for st in range(3):
        for k in range(3):
            ar_copy(st, k).wait_send()

    def drain(i, _):
        x_copy(i).wait_send()
        for k in range(2):
            z1_copy(i, k).wait_send()
            z2_copy(i, k).wait_send()
        for r in range(1, 8):
            y_copy(i, r).wait_send()
        d_copy(i).wait_send()
        return 0

    lax.fori_loop(0, 6, drain, 0)


def on_device(shifted, out_grad, conv_weight, norm_gain, norm_bias, shift_fwd, shift_bwd):
    scale = 131072.0 ** (-0.5)
    x = shifted.reshape(1024, CH)
    g = out_grad.reshape(4, 256, CH)
    wp = conv_weight.reshape(10, 3, 3, 2, HALF).transpose(3, 1, 0, 2, 4).reshape(2, 3, 10, 3 * HALF)
    wp = jnp.pad(wp, ((0, 0), (0, 0), (0, 0), (0, WIDE - 3 * HALF)))
    wp = wp.reshape(2, 3, 10, 8, 128).transpose(0, 3, 1, 2, 4).reshape(2, 240, 128)
    pad = lambda v: jnp.pad(v, (0, 48), constant_values=-1).reshape(1, 128)
    dma = pltpu.SemaphoreType.DMA
    vm = pltpu.VMEM
    scratch = [
        vm((2, 1024, HALF), bf16), vm((1024, HALF), bf16), vm((8, 288, CH), bf16), vm((CH, 2048), bf16),
        vm((CH, CH), bf16), vm((8, 288, WIDE), bf16), vm((8, 240, 128), bf16), vm((3, 8, 80, WIDE), bf16),
        vm((2048, WIDE), f32), vm((2048, HALF), f32),
        vm((8, HALF), f32), vm((8, HALF), f32), vm((8, HALF), f32), vm((8, HALF), f32), vm((8, HALF), f32), vm((8, HALF), f32),
        vm((6, HALF, 512), f32), vm((6, HALF, 512), bf16), vm((6, HALF, 512), bf16),
        vm((6, 2, 80, 256), bf16), vm((6, 2, 80, 256), bf16), vm((6, 2, 80, 512), bf16), vm((6, 2, 80, 512), bf16),
        vm((6, 8, 16, 512), f32), vm((6, 8, 16, 512), bf16), vm((6, 8, 16, 512), bf16),
        vm((6, 2, 16, 512), f32), vm((6, 2, 16, 512), f32),
        vm((10, 256, HALF), bf16), vm((4, 256, HALF), bf16), vm((4, 256, HALF), bf16),
        vm((2, 256, 128), bf16), vm((2, 256, 128), bf16), vm((2, HALF, 128), bf16),
        vm((3, 8, HALF), f32), vm((3, 3, 8, HALF), f32), vm((2, 8, HALF), f32),
        dma((1,)), dma((4,)), dma((4,)), dma((7,)), dma((7,)), dma((2, 4)), dma((2, 4)), dma((4,)), dma((4,)),
        dma((4, 2)), dma((4, 2)), dma((4, 2)), dma((4, 2)),
        dma((6,)), dma((6,)), dma((6, 2)), dma((6, 2)), dma((6, 2)), dma((6, 2)), dma((6, 8)), dma((6, 8)),
        dma((6,)), dma((6,)), dma((2,)), dma((2,)), dma((3, 3)), dma((3, 3)),
    ]
    v = pl.BlockSpec(memory_space=pltpu.VMEM)

    def body(*refs):
        kernel(scale, *refs)

    ig, wg, gb = pl.pallas_call(
        body,
        out_shape=(
            jax.ShapeDtypeStruct((1024, CH), bf16),
            jax.ShapeDtypeStruct((2, 3, 16, WIDE), f32),
            jax.ShapeDtypeStruct((2, 8, HALF), f32),
        ),
        in_specs=[v, pl.BlockSpec(memory_space=pl.ANY), v, v, v, v, v],
        out_specs=(v, v, v),
        scratch_shapes=scratch,
        compiler_params=pltpu.CompilerParams(collective_id=0, has_side_effects=True, vmem_limit_bytes=60 << 20),
    )(x, g, wp, norm_gain.reshape(1, CH), norm_bias.reshape(1, CH), pad(shift_fwd), pad(shift_bwd))
    wg = wg[:, :, :10, : 3 * HALF].reshape(2, 3, 10, 3, HALF).transpose(2, 1, 3, 0, 4).reshape(10, 9 * CH)
    return (ig.reshape(shifted.shape), wg, gb[:, 0].reshape(CH), gb[:, 1].reshape(CH))


def solution(mesh):
    in_specs = (
        P("dp", "frames", None, None, None),
        P("dp", "frames", None, None, None),
        P("frames", None),
        P(),
        P(),
        P(),
        P(),
    )
    out_specs = (P("dp", "frames", None, None, None), P("frames", None), P(), P())
    return jax.shard_map(
        on_device, mesh=mesh, in_specs=in_specs, out_specs=out_specs, check_vma=False
    )
```

time: 929 us -> 105 us (0.11)
  waiting for transfers between devices: 678 us -> 0 us
  Pallas kernels: 0 us -> 93.7 us
  local copies, waits for them, and re-layouts: 81.4 us -> 10.6 us
  blocking collectives: 67.9 us -> 0 us
  matrix products: 45.7 us -> 0 us
  other arithmetic: 29.7 us -> 0 us
  between operations: 15 us -> 0.73 us
    unnamed x4 -> x0, waiting for transfers between devices: 517 us -> none
    pallas_call x0 -> x1, Pallas kernels: none -> 93.7 us  [on_device(): pl.pallas_call(body, out_shape=(jax.ShapeDtypeStruct((1024, CH), bf16), j...]
    psum x1 -> x0, waiting for transfers between devices: 82.4 us -> none  [on_device(): kernel_shard = lax.psum(kernel_shard, 'dp')]
    all_gather x1 -> x0, waiting for transfers between devices: 78.7 us -> none  [on_device(): whole_weight = lax.all_gather(conv_weight, 'frames', axis=0, tiled=True)]
    psum x1 -> x0, blocking collectives: 67.9 us -> none  [on_device(): gain_total, bias_total = lax.psum((gain_part, bias_part), ('frames', 'dp'))]
    dot_general x22 -> x0, matrix products: 45.7 us -> none  [the longest x9 21.8 us: on_device(): lax.dot_general(grad_rows, act_view, (((0,), (0,)), ((), ())), preferred_...]
    convert_element_type x2 -> x0, local copies, waits for them, and re-layouts: 33.4 us -> none  [on_device(): frames_local.astype(jnp.float32)]
    unnamed x38 -> x7, local copies, waits for them, and re-layouts: 25.6 us -> 1.07 us
  transfers between devices with their start and end apart: 5 -> 0, of which waited for: 3 -> 0; matrix products, arithmetic and copies ran while one was open for 6% -> 0% of each run, Pallas kernels for 0% -> 0%
where the time goes in v1:
time: 105 us
  Pallas kernels  93.7 us (89%)
  local copies, waits for them, and re-layouts  10.6 us (10%)
    pallas_call x1, Pallas kernels, on_device(): pl.pallas_call(body, out_shape=(jax.ShapeDtypeStruct((1024, CH), bf16), j...  93.7 us

profile of v1, /device:TPU:1, one launch (start us, length us, event | category | flops | bytes accessed | tf_op | source)
XLA Modules:
  0.0 105.0 jit_solution(9487470801410855811)
XLA Ops:
  0.6 0.0 copy-start.1
  0.6 0.0 copy-start.2
  0.7 1.2 %pad_bitcast_fusion = (s32[1,128]{1,0:T(1,128)}, s32[1,128]{1,0:T(1,128)}) fusion(s32[80]{0:T(128)} %param.13, s32[80]{0:T(128)} %param.12), kind=kLoop, calls=%fused_computation.3 | loop fusion | bytes 1664 | tf_op jit(solution)/shard_map/reshape | solution.py:562
  1.8 1.2 %reshape.49 = bf16[10,3,3,2,320]{4,3,2,1,0:T(2,128)(2,1)S(1)} reshape(bf16[10,5760]{1,0:T(8,128)(2,1)} %param.9) | data formatting | bytes 230400 | tf_op jit(solution)/shard_map/reshape | solution.py:559
  3.0 0.1 copy.22
  3.1 0.2 reshape.50
  3.3 0.1 pad.11
  3.4 0.1 reshape.51
  3.5 0.1 copy.17
  3.6 0.7 copy.18.refs_2_
  4.2 0.0 copy-done.1
  4.2 0.6 reshape.53.refs_3_
  4.8 0.0 copy-done.2
  4.8 0.6 reshape.54.refs_4_
  5.4 93.7 %shard_map.102 = (bf16[1024,640]{1,0:T(8,128)(2,1)}, f32[2,3,16,1024]{3,2,1,0:T(8,128)}, f32[2,8,320]{2,1,0:T(8,128)}) custom-call(bf16[1024,640]{1,0:T(8,128)(2,1)} %bitcast.21, bf16[4,256,640]{2,1,0:T(8,128)(2,1)} %bitcast.22, bf16[2,240,128]{2,1,0:T(8,128)(2,1)} %copy.18.refs_2_, f32[1,640]{1,0:T(1,128)} %reshape.53.refs_3_, f32[1,640]{1,0:T(1,128)} %reshape.54.refs_4_, ...), custom_call_target="tpu_custom_call" | custom-call | tf_op jit(solution)/shard_map/pallas_call | solution.py:587
  99.1 0.0 copy-start
  99.1 0.9 slice_reduce_fusion
  100.0 0.7 reshape_squeeze.6
  100.7 0.7 reshape_squeeze.7
  101.3 1.2 %copy.19 = f32[2,3,10,960]{3,0,2,1:T(2,128)S(1)} copy(f32[2,3,10,960]{3,2,1,0:T(8,128)} %bitcast.27) | data formatting | bytes 460800 | tf_op jit(solution)/shard_map/slice | solution.py:599
  102.5 0.3 reshape.58
  102.8 0.1 copy.20
  103.0 1.0 reshape.59
  104.0 1.1 %copy.24 = bf16[1,4,16,16,640]{4,3,2,1,0:T(8,128)(2,1)} copy(bf16[1,4,16,16,640]{4,3,2,1,0:T(8,128)(2,1)S(1)} %bitcast.23) | data formatting | bytes 2621440
  (1 shorter events, 0.0 us)
Async XLA Ops:
  0.6 3.6 %copy-start.1 = (f32[640]{0:T(1024)S(1)}, f32[640]{0:T(1024)}, u32[]{:S(2)}) copy-start(f32[640]{0:T(1024)} %param.10) | copy-start | bytes 7684
  0.6 4.2 %copy-start.2 = (f32[640]{0:T(1024)S(1)}, f32[640]{0:T(1024)}, u32[]{:S(2)}) copy-start(f32[640]{0:T(1024)} %param.11) | copy-start | bytes 7684
  99.1 4.9 %copy-start = (bf16[1024,640]{1,0:T(8,128)(2,1)S(1)}, bf16[1024,640]{1,0:T(8,128)(2,1)}, u32[]{:S(2)}) copy-start(bf16[1024,640]{1,0:T(8,128)(2,1)} %get-tuple-element.7) | copy-start | bytes 3932164

commit v2 on v1

v2 whole, which is shorter than its diff:
```python
import jax
import jax.numpy as jnp
from jax import lax
from jax.experimental import pallas as pl
from jax.experimental.pallas import tpu as pltpu
from jax.sharding import PartitionSpec as P

f32, bf16 = jnp.float32, jnp.bfloat16
MESH = pl.DeviceIdType.MESH
EPS = 1e-05
CH, HALF, WIDE = 640, 320, 1024
HIGH = lax.Precision.HIGHEST


def dot(a, b):
    return jnp.dot(a, b, preferred_element_type=f32)


def dot_nt(a, b):
    return lax.dot_general(a, b, (((1,), (1,)), ((), ())), preferred_element_type=f32)


def rows16(v, n):
    return pl.ds(pl.multiple_of(v, 16), n)


def div20(i):
    return (i * 3277) >> 16


def kernel(
    scale,
    x_hbm, g_hbm, w_ref, gain_ref, bias_ref, fwd_ref, bwd_ref,
    ig_ref, fin, gb_ref,
    wpc, x_ref, xs, xb, gp, gt, pm, ap, p1, w, y_acc, pre,
    cen, inv, s1, s2, m1, m2,
    s_buf, wgs, xr, zs, zr, yf, ys, yr, ds_, dr,
    sgp, igs, igr, hs, hr, selm, a1s, a1r, a2s, a2r,
    loc_sem, ex_s, ex_r, p1_s, p1_r, zo_s, zo_r, zf_s, zf_r, cr_s, cr_r, yi_s, yi_r,
    x_s, x_r, z_ss, z_rs, y_ss, y_rs, d_ss, d_rs, h_ss, h_rs, a1_ss, a1_rs, a2_ss, a2_rs,
):
    f = lax.axis_index("frames")
    d = lax.axis_index("dp")
    c = f % 2
    xl = (f // 2) % 2
    y = (f // 4) % 4
    z = f // 16
    x = d * 2 + xl
    y0 = y % 2
    y1 = y // 2

    def dev(zz, yy, xx, cc):
        return {"frames": ((zz * 4 + yy) * 2 + xx % 2) * 2 + cc, "dp": xx // 2}

    oc = 1 - c
    zp, zm, zo = (z + 1) % 4, (z + 3) % 4, (z + 2) % 4
    yin = y + 1 - 2 * y0
    ycross = (y + 3 + 2 * y0) % 4
    xin = x + 1 - 2 * xl
    xcross = (x + 3 + 2 * xl) % 4
    xop = (x + 2) % 4
    sib = dev(z, y, x, oc)
    nxt = {"frames": (f + 2) % 64, "dp": d}
    prv = {"frames": (f + 62) % 64, "dp": d}

    def remote(src, dst, ss, rs, to):
        return pltpu.make_async_remote_copy(
            src_ref=src, dst_ref=dst, send_sem=ss, recv_sem=rs, device_id=to, device_id_type=MESH
        )

    barrier = pltpu.get_barrier_semaphore()
    partners = [sib, nxt, prv]
    for yy, xx in ((yin, x), (y, xin), (yin, xin)):
        partners += [dev(z, yy, xx, 0), dev(z, yy, xx, 1)]
    for k in (2, 3):
        yy = (ycross, (y + 2) % 4)[k - 2]
        partners += [dev(z, yy, x, 0), dev(z, yy, x, 1)]
    for xx in (xcross, xop):
        partners += [dev(z, y, xx, 0), dev(z, y, xx, 1)]
    partners += [dev(zz, (y + dy) % 4, x, c) for zz in (zp, zm, zo) for dy in range(4)]
    for to in partners:
        pl.semaphore_signal(barrier, inc=1, device_id=to, device_id_type=MESH)

    x_local = pltpu.make_async_copy(x_hbm, x_ref, loc_sem.at[1])
    x_local.start()
    for h in range(2):
        wide = []
        for a in range(3):
            taps = [w_ref[:, (3 * a + b) * CH + h * HALF : (3 * a + b) * CH + (h + 1) * HALF].astype(f32) for b in range(3)]
            wide.append(jnp.concatenate(taps + [jnp.zeros((10, WIDE - 3 * HALF), f32)], axis=1))
        pieces = [wide[a][:, lb * 128 : lb * 128 + 128] for lb in range(8) for a in range(3)]
        wpc[h] = jnp.concatenate(pieces, axis=0).astype(bf16)
    pl.semaphore_wait(barrier, len(partners))
    me8 = (y0 * 2 + xl) * 2 + c
    p1c = []
    k = 0
    for yy, xx, dc in ((y, x, 1), (y, xin, 0), (y, xin, 1), (yin, x, 0), (yin, x, 1), (yin, xin, 0), (yin, xin, 1)):
        cc = c + dc - 2 * c * dc
        p1c.append(remote(wpc.at[cc], p1.at[me8], p1_s.at[k], p1_r.at[k], dev(z, yy, xx, cc)))
        k += 1
    for cp in p1c:
        cp.start()
    interior = (pl.ds(c * 4, 4), pl.ds(16, 256))
    g_local = pltpu.make_async_copy(g_hbm, gp.at[interior], loc_sem.at[0])
    g_remote = remote(g_hbm, gp.at[interior], ex_s.at[0], ex_r.at[0], sib)
    g_local.start()
    p1[me8] = wpc[c]

    x_local.wait()
    def split(t, _):
        r = rows16(t * 256, 256)
        v = x_ref[r, :].astype(f32)
        xs[0, r, :] = v[:, :HALF].astype(bf16)
        xs[1, r, :] = v[:, HALF:].astype(bf16)
        return 0

    lax.fori_loop(0, 4, split, 0)
    x_remote = remote(xs.at[oc], xb, ex_s.at[1], ex_r.at[1], sib)
    x_remote.start()
    g_remote.start()

    def read_x(t):
        r = rows16((t % 4) * 256, 256)
        mine = xs[c, r, :]
        other = xb[r, :]
        return jnp.where(t // 4 == c, mine, other).astype(f32)

    zero16 = jnp.zeros((16, CH), bf16)
    zero16w = jnp.zeros((16, WIDE), bf16)
    for t in range(8):
        gp[t, 0:16, :] = zero16
        gp[t, 272:288, :] = zero16
        ap[t, 0:16, :] = zero16w
        ap[t, 272:288, :] = zero16w

    oi = lax.broadcasted_iota(jnp.int32, (CH, CH), 0)
    li = lax.broadcasted_iota(jnp.int32, (CH, CH), 1)
    q = (oi >= HALF).astype(jnp.int32)
    rr = oi - HALF * q
    zy = div20(rr)
    src_row = (2 * zy + (q + xl - 2 * q * xl)) * 20 + (rr - 20 * zy)
    pm[...] = (li == src_row).astype(f32).astype(bf16)
    gi = div20(lax.broadcasted_iota(jnp.int32, (HALF, HALF), 0))
    gj = div20(lax.broadcasted_iota(jnp.int32, (HALF, HALF), 1))
    group_mean = jnp.where(gi == gj, 1.0 / 5120.0, 0.0).astype(f32)

    def spread_groups(v):
        return jnp.dot(v, group_mean, preferred_element_type=f32, precision=HIGH)

    mine0 = c == 0
    gain_all, bias_all = gain_ref[...].reshape(1, CH), bias_ref[...].reshape(1, CH)
    gain = jnp.where(mine0, gain_all[:, :HALF], gain_all[:, HALF:])
    bias = jnp.where(mine0, bias_all[:, :HALF], bias_all[:, HALF:])

    def transpose(t):
        gt[:, pl.ds(pl.multiple_of(t * 256, 256), 256)] = dot_nt(pm[...], gp[t, 16:272, :]).astype(bf16)

    g_local.wait()

    def transpose_mine(i, _):
        transpose(c * 4 + i)
        return 0

    lax.fori_loop(0, 4, transpose_mine, 0)

    for cp in p1c:
        cp.wait_recv()
    blk = z * 2 + y1
    oblk = 1 - 2 * y1
    for lb in range(8):
        for a in range(3):
            r = (lb * 3 + a) * 10
            piece = jnp.concatenate([p1[s, r : r + 10, :].astype(f32) for s in range(8)], axis=0)
            w[a, blk, :, lb * 128 : lb * 128 + 128] = piece.astype(bf16)

    def lanes(qq, n=256):
        return pl.ds(pl.multiple_of(qq * 256, 256), n)

    def wsl(b, qq):
        return w.at[:, b, :, lanes(qq)]

    def quarter(j):
        return (2 * (j % 2) + 1 - y0) if j < 2 else (2 * (j % 2) + y0)

    def z_own(k, j):
        s = wsl(blk, quarter(j))
        return remote(s, s, zo_s.at[k, j], zo_r.at[k, j], dev((zp, zm)[k], y, x, c))

    def z_fwd(j):
        up = j % 2 == 0
        s = wsl((zm if up else zp) * 2 + y1, quarter(j))
        return remote(s, s, zf_s.at[j], zf_r.at[j], dev(zp if up else zm, y, x, c))

    zrel = (z, zm, zp, zo)

    def cross(k, h):
        s = wsl(zrel[k] * 2 + y1, 2 * h + 1 - y0)
        return remote(s, s, cr_s.at[k, h], cr_r.at[k, h], dev(z, ycross, x, c))

    def inner(k, h):
        s = wsl(zrel[k] * 2 + 1 - y1, 2 * h + y0)
        return remote(s, s, yi_s.at[k, h], yi_r.at[k, h], dev(z, yin, x, c))

    def z_start(j):
        z_own(0, j).start()
        z_own(1, j).start()

    def z_wait(j):
        z_own(0, j).wait_recv()
        z_own(1, j).wait_recv()

    def hook_in(k, h):
        cross(k, h).wait_recv()
        inner(k, h).start()

    def hook0():
        z_start(1)
        cross(0, 1).start()

    def hook1():
        z_wait(0)
        z_fwd(0).start()
        cross(1, 0).start()
        hook_in(0, 0)

    def hook2():
        cross(2, 0).start()
        z_start(2)

    def hook3():
        z_wait(1)
        z_fwd(1).start()
        cross(1, 1).start()
        hook_in(0, 1)

    def hook4():
        z_fwd(0).wait_recv()
        cross(3, 0).start()
        hook_in(1, 0)
        z_start(3)

    def hook5():
        hook_in(2, 0)
        cross(2, 1).start()

    def hook6():
        z_wait(2)
        z_fwd(2).start()
        z_fwd(1).wait_recv()
        cross(3, 1).start()

    def hook7():
        hook_in(3, 0)
        z_wait(3)
        z_fwd(3).start()

    def hook8():
        hook_in(1, 1)

    cross(0, 0).start()
    z_start(0)

    x_remote.wait_recv()

    def stat_sum(t, _):
        s1[pl.ds(t, 1), :] = jnp.sum(read_x(t), axis=0, keepdims=True)
        return 0

    lax.fori_loop(0, 8, stat_sum, 0)
    cen[...] = spread_groups(s1[...])

    def stat_sq(t, _):
        v = read_x(t) - cen[pl.ds(t, 1), :]
        s2[pl.ds(t, 1), :] = jnp.sum(v * v, axis=0, keepdims=True)
        return 0

    lax.fori_loop(0, 8, stat_sq, 0)
    inv[...] = lax.rsqrt(spread_groups(s2[...]) + EPS)

    col = lax.broadcasted_iota(jnp.int32, (256, HALF), 0) % 16

    def normed_of(t):
        return (read_x(t) - cen[pl.ds(t, 1), :]) * inv[pl.ds(t, 1), :]

    def forward(t, _):
        before = normed_of(t) * gain + bias
        act = before / (1.0 + jnp.exp(-before))
        left = jnp.where(col == 0, 0.0, pltpu.roll(act, 1, 0))
        right = jnp.where(col == 15, 0.0, pltpu.roll(act, 255, 0))
        cat = jnp.concatenate([left, act, right, jnp.zeros((256, WIDE - 3 * HALF), f32)], axis=1)
        ap[t, 16:272, :] = cat.astype(bf16)
        return 0

    lax.fori_loop(0, 2, forward, 0)
    hook0()
    lax.fori_loop(2, 8, forward, 0)
    hook1()
    g_remote.wait_recv()

    def transpose_other(i, _):
        transpose(oc * 4 + i)
        return 0

    lax.fori_loop(0, 4, transpose_other, 0)
    hook2()

    def x_copy(i, k):
        to = (xin, xcross)[k]
        return remote(wgs.at[i, k], xr.at[i, k], x_s.at[i, k], x_r.at[i, k], dev(z, y, to, c))

    def wg_step(i, _):
        a, n = i // 2, i % 2
        cols = pl.ds(pl.multiple_of(n * 512, 512), 512)
        acc = None
        for t in range(8):
            v = dot(gt[:, t * 256 : t * 256 + 256], ap[t, rows16(a * 16, 256), cols])
            acc = v if acc is None else acc + v
        s_buf[i] = acc[:HALF, :]
        wgs[i, 0] = acc[HALF:, :256].astype(bf16)
        wgs[i, 1] = acc[HALF:, 256:].astype(bf16)
        x_copy(i, 0).start()
        x_copy(i, 1).start()

        for k, hook in enumerate((hook3, hook4, hook5, hook6, hook7, hook8)):
            pl.when(i == k)(hook)
        pl.when(i == 4)(lambda: stage1(0))
        return 0

    def z_copy(i, k):
        return remote(zs.at[i, k], zr.at[i, k], z_ss.at[i, k], z_rs.at[i, k], dev((zp, zm, zo)[k], y, x, c))

    def y_copy(i, r):
        dy, dc = r // 2, r % 2
        yy, cc = (y + dy) % 4, c + dc - 2 * c * dc
        return remote(ys.at[i, yy * 2 + cc], yr.at[i, r], y_ss.at[i, r], y_rs.at[i, r], dev(z, yy, x, cc))

    def d_copy(i):
        return remote(ds_.at[i], dr.at[i], d_ss.at[i], d_rs.at[i], dev(z, y, xop, c))

    def block(b):
        return rows16(b * 80, 80)

    def stage1(i):
        x_copy(i, 0).wait_recv()
        x_copy(i, 1).wait_recv()
        s_buf[i, :, :256] = s_buf[i, :, :256] + xr[i, 0].astype(f32)
        s_buf[i, :, 256:] = s_buf[i, :, 256:] + xr[i, 1].astype(f32)
        for k in range(3):
            zs[i, k] = s_buf[i, block((zp, zm, zo)[k]), :].astype(bf16)
            z_copy(i, k).start()

    def stage2(i):
        total = s_buf[i, block(z), :]
        for k in range(3):
            z_copy(i, k).wait_recv()
            total = total + zr[i, k].astype(f32)
        total = jnp.concatenate([total, jnp.zeros((8, 512), f32)], axis=0)
        for k in range(8):
            piece = total[10 * k : 10 * k + 16, :]
            yf[i, k] = piece
            ys[i, k] = piece.astype(bf16)
        for r in range(1, 8):
            y_copy(i, r).start()

    def stage3(i):
        for r in range(1, 8):
            y_copy(i, r).wait_recv()
        own = yf[i, y * 2 + c]
        for dy in (1, 2, 3):
            own = own + yr[i, 2 * dy].astype(f32)
        other = yr[i, 1].astype(f32)
        for dy in (1, 2, 3):
            other = other + yr[i, 2 * dy + 1].astype(f32)
        ds_[i, 0] = own
        ds_[i, 1] = other
        d_copy(i).start()

    def stage4(i):
        d_copy(i).wait_recv()
        own = (ds_[i, 0] + dr[i, 0]) * scale
        other = (ds_[i, 1] + dr[i, 1]) * scale
        a, n = i // 2, i % 2
        cols = pl.ds(pl.multiple_of(n * 512, 512), 512)
        fin[0, a, :, cols] = jnp.where(mine0, own, other)
        fin[1, a, :, cols] = jnp.where(mine0, other, own)

    lax.fori_loop(0, 6, wg_step, 0)
    stage1(1)
    for k in range(4):
        inner(k, 0).wait_recv()
    z_fwd(2).wait_recv()

    def back1(t, _):
        r = rows16(t * 256, 256)
        v = y_acc[r, :]
        right = jnp.where(col == 15, 0.0, pltpu.roll(v[:, :HALF], 255, 0))
        left = jnp.where(col == 0, 0.0, pltpu.roll(v[:, 2 * HALF : 3 * HALF], 1, 0))
        act_grad = right + v[:, HALF : 2 * HALF] + left
        normed = normed_of(t)
        before = normed * gain + bias
        g = 1.0 / (1.0 + jnp.exp(-before))
        p = act_grad * g * (1.0 + before * (1.0 - g))
        pre[r, :] = p
        s1[pl.ds(t, 1), :] = jnp.sum(p * normed, axis=0, keepdims=True)
        s2[pl.ds(t, 1), :] = jnp.sum(p, axis=0, keepdims=True)
        return 0

    def back2(t, _):
        r = rows16(t * 256, 256)
        v = pre[r, :] * gain - m1[pl.ds(t, 1), :] - normed_of(t) * m2[pl.ds(t, 1), :]
        sgp[t + 1] = (v * inv[pl.ds(t, 1), :]).astype(bf16)
        return 0

    def back1_of(frames):
        for t in frames:
            back1(t, 0)

    def group_terms():
        m1[...] = spread_groups(s2[...] * gain)
        m2[...] = spread_groups(s1[...] * gain)

    halo = [
        remote(hs.at[0], hr.at[0], h_ss.at[0], h_rs.at[0], nxt),
        remote(hs.at[1], hr.at[1], h_ss.at[1], h_rs.at[1], prv),
    ]
    ch_id = lax.broadcasted_iota(jnp.int32, (HALF, 80), 0) + c * HALF
    selm[0] = (ch_id == bwd_ref[...].reshape(1, 80)).astype(f32).astype(bf16)
    selm[1] = (ch_id == fwd_ref[...].reshape(1, 80)).astype(f32).astype(bf16)

    def edge_frames():
        back1_of((0, 1, 6, 7))
        group_terms()
        back2(0, 0)
        back2(7, 0)
        hs[0] = dot(sgp[8], selm[0]).astype(bf16)
        hs[1] = dot(sgp[1], selm[1]).astype(bf16)
        halo[0].start()
        halo[1].start()

    def act_step(i, _):
        n = i // 4
        tt = (i + 3 * n) % 4

        @pl.when(i == 4)
        def _():
            for k in range(4):
                inner(k, 1).wait_recv()
            z_fwd(3).wait_recv()

        cols = pl.ds(pl.multiple_of(n * 512, 512), 512)
        lhs = jnp.concatenate(
            [
                jnp.concatenate([gp[tt * 2 + t, 16 * (2 - a) : 16 * (2 - a) + 256, :] for a in range(3)], axis=1)
                for t in range(2)
            ],
            axis=0,
        )
        rhs = w[:, :, :, cols].reshape(3 * CH, 512)
        y_acc[rows16(tt * 512, 512), cols] = dot(lhs, rhs)
        plan = {
            0: [(stage1, 2)],
            1: [],
            2: [(stage2, 0), (stage1, 3)],
            3: [(stage2, 1)],
            4: [(stage1, 4)],
            5: [(stage3, 0), (stage2, 2), (stage1, 5)],
            6: [(stage3, 1), (stage2, 3)],
            7: [(stage3, 2), (stage2, 4)],
        }
        for k, work in plan.items():

            @pl.when(i == k)
            def _(k=k, work=work):
                if k < 2:
                    hook_in(k + 2, 1)
                for stage, chunk in work:
                    stage(chunk)

        pl.when(i == 5)(edge_frames)
        return 0

    lax.fori_loop(0, 8, act_step, 0)

    def a1_copy(r):
        dx, dc = r // 2, r % 2
        cc = c + dc - 2 * c * dc
        return remote(a1s, a1r.at[r], a1_ss.at[r], a1_rs.at[r], dev(z, y, (x + dx) % 4, cc))

    def a2_copy(r):
        return remote(a2s, a2r.at[r], a2_ss.at[r], a2_rs.at[r], dev((z + r // 4) % 4, (y + r % 4) % 4, x, c))

    back1_of((2, 3, 4, 5))
    total = [jnp.sum(v[...], axis=0, keepdims=True) for v in (s1, s2)]
    a1s[...] = jnp.concatenate(total + [jnp.zeros((6, HALF), f32)], axis=0)
    for r in range(1, 8):
        a1_copy(r).start()
    stage2(5)
    group_terms()
    lax.fori_loop(1, 7, back2, 0)
    stage3(3)
    halo[0].wait_recv()
    halo[1].wait_recv()
    keep_prev = jnp.where(f >= 2, 1.0, 0.0)
    keep_next = jnp.where(f < 62, 1.0, 0.0)
    sgp[0] = (dot_nt(hr[0], selm[0]) * keep_prev).astype(bf16)
    sgp[9] = (dot_nt(hr[1], selm[1]) * keep_next).astype(bf16)
    ones = jnp.ones((8, 80), bf16)
    bwd_mask = dot_nt(ones, selm[0])[0:1, :] > 0.5
    fwd_mask = dot_nt(ones, selm[1])[0:1, :] > 0.5

    def shift(t):
        v = jnp.where(bwd_mask, sgp[t].astype(f32), sgp[t + 1].astype(f32))
        return jnp.where(fwd_mask, sgp[t + 2].astype(f32), v)

    def shift_other(i, _):
        igs[i] = shift(oc * 4 + i).astype(bf16)
        return 0

    lax.fori_loop(0, 4, shift_other, 0)
    i_copy = remote(igs, igr, ex_s.at[2], ex_r.at[2], sib)
    i_copy.start()
    stage3(4)
    for r in range(1, 8):
        a1_copy(r).wait_recv()
    own = a1s[0:2, :]
    for r in (2, 4, 6):
        own = own + a1r[r, 0:2, :]
    other = a1r[1, 0:2, :]
    for r in (3, 5, 7):
        other = other + a1r[r, 0:2, :]
    a2s[...] = jnp.concatenate([own, other, jnp.zeros((4, HALF), f32)], axis=0)
    for r in range(1, 16):
        a2_copy(r).start()
    stage3(5)

    def keep(i, _):
        ig_ref[c, rows16(i * 256, 256), :] = shift(c * 4 + i).astype(bf16)
        return 0

    lax.fori_loop(0, 4, keep, 0)
    i_copy.wait_recv()
    ig_ref[oc] = igr[...].reshape(1024, HALF)
    for i in range(5):
        stage4(i)
    total = a2s[...]
    for r in range(1, 16):
        a2_copy(r).wait_recv()
        total = total + a2r[r]
    total = total * scale
    gb_ref[c, 0:2, :] = total[0:2, :]
    gb_ref[oc, 0:2, :] = total[2:4, :]
    stage4(5)

    for cp in p1c:
        cp.wait_send()
    for cp in (g_remote, x_remote, i_copy, halo[0], halo[1]):
        cp.wait_send()
    for qq in range(4):
        z_own(0, qq).wait_send()
        z_own(1, qq).wait_send()
        z_fwd(qq).wait_send()
    for k in range(4):
        for h in range(2):
            cross(k, h).wait_send()
            inner(k, h).wait_send()
    for r in range(1, 8):
        a1_copy(r).wait_send()
    for r in range(1, 16):
        a2_copy(r).wait_send()

    def drain(i, _):
        for k in range(2):
            x_copy(i, k).wait_send()
        for k in range(3):
            z_copy(i, k).wait_send()
        for r in range(1, 8):
            y_copy(i, r).wait_send()
        d_copy(i).wait_send()
        return 0

    lax.fori_loop(0, 6, drain, 0)


def join_halves(ig_ref, fin, gb_ref, out_ref, wg_ref, gg_ref, bg_ref):
    def rows(i, _):
        r = rows16(i * 256, 256)
        both = jnp.concatenate([ig_ref[0, r, :].astype(f32), ig_ref[1, r, :].astype(f32)], axis=1)
        out_ref[r, :] = both.astype(bf16)
        return 0

    lax.fori_loop(0, 4, rows, 0)
    for a in range(3):
        for b in range(3):
            tap = jnp.concatenate([fin[h, a, 0:10, b * HALF : (b + 1) * HALF] for h in range(2)], axis=1)
            wg_ref[:, (3 * a + b) * CH : (3 * a + b + 1) * CH] = tap
    both = jnp.concatenate([gb_ref[0, 0:2, :], gb_ref[1, 0:2, :]], axis=1)
    gg_ref[...] = both[0:1, :].reshape(CH)
    bg_ref[...] = both[1:2, :].reshape(CH)


def on_device(shifted, out_grad, conv_weight, norm_gain, norm_bias, shift_fwd, shift_bwd):
    scale = 131072.0 ** (-0.5)
    x = shifted.reshape(1024, CH)
    g = out_grad.reshape(4, 256, CH)
    dma = pltpu.SemaphoreType.DMA
    vm = pltpu.VMEM
    scratch = [
        vm((2, 240, 128), bf16), vm((1024, CH), bf16),
        vm((2, 1024, HALF), bf16), vm((1024, HALF), bf16), vm((8, 288, CH), bf16), vm((CH, 2048), bf16),
        vm((CH, CH), bf16), vm((8, 288, WIDE), bf16), vm((8, 240, 128), bf16), vm((3, 8, 80, WIDE), bf16),
        vm((2048, WIDE), f32), vm((2048, HALF), f32),
        vm((8, HALF), f32), vm((8, HALF), f32), vm((8, HALF), f32), vm((8, HALF), f32), vm((8, HALF), f32), vm((8, HALF), f32),
        vm((6, HALF, 512), f32), vm((6, 2, HALF, 256), bf16), vm((6, 2, HALF, 256), bf16),
        vm((6, 3, 80, 512), bf16), vm((6, 3, 80, 512), bf16),
        vm((6, 8, 16, 512), f32), vm((6, 8, 16, 512), bf16), vm((6, 8, 16, 512), bf16),
        vm((6, 2, 16, 512), f32), vm((6, 2, 16, 512), f32),
        vm((10, 256, HALF), bf16), vm((4, 256, HALF), bf16), vm((4, 256, HALF), bf16),
        vm((2, 256, 80), bf16), vm((2, 256, 80), bf16), vm((2, HALF, 80), bf16),
        vm((8, HALF), f32), vm((8, 8, HALF), f32), vm((8, HALF), f32), vm((16, 8, HALF), f32),
        dma((2,)), dma((4,)), dma((4,)), dma((7,)), dma((7,)), dma((2, 4)), dma((2, 4)), dma((4,)), dma((4,)),
        dma((4, 2)), dma((4, 2)), dma((4, 2)), dma((4, 2)),
        dma((6, 2)), dma((6, 2)), dma((6, 3)), dma((6, 3)), dma((6, 8)), dma((6, 8)),
        dma((6,)), dma((6,)), dma((2,)), dma((2,)), dma((8,)), dma((8,)), dma((16,)), dma((16,)),
    ]
    v = pl.BlockSpec(memory_space=pltpu.VMEM)

    def body(*refs):
        kernel(scale, *refs)

    parts = pl.pallas_call(
        body,
        out_shape=(
            jax.ShapeDtypeStruct((2, 1024, HALF), bf16),
            jax.ShapeDtypeStruct((2, 3, 16, WIDE), f32),
            jax.ShapeDtypeStruct((2, 8, HALF), f32),
        ),
        in_specs=[pl.BlockSpec(memory_space=pl.ANY), pl.BlockSpec(memory_space=pl.ANY), v, v, v, v, v],
        out_specs=(v, v, v),
        scratch_shapes=scratch,
        compiler_params=pltpu.CompilerParams(collective_id=0, has_side_effects=True, vmem_limit_bytes=60 << 20),
    )(x, g, conv_weight, norm_gain, norm_bias, shift_fwd, shift_bwd)
    ig, wg, gg, bg = pl.pallas_call(
        join_halves,
        out_shape=(
            jax.ShapeDtypeStruct((1024, CH), bf16),
            jax.ShapeDtypeStruct((10, 9 * CH), f32),
            jax.ShapeDtypeStruct((CH,), f32),
            jax.ShapeDtypeStruct((CH,), f32),
        ),
        in_specs=[v, v, v],
        out_specs=(v, v, v, v),
    )(*parts)
    return (ig.reshape(shifted.shape), wg, gg, bg)


def solution(mesh):
    in_specs = (
        P("dp", "frames", None, None, None),
        P("dp", "frames", None, None, None),
        P("frames", None),
        P(),
        P(),
        P(),
        P(),
    )
    out_specs = (P("dp", "frames", None, None, None), P("frames", None), P(), P())
    return jax.shard_map(
        on_device, mesh=mesh, in_specs=in_specs, out_specs=out_specs, check_vma=False
    )
```

time: 105 us -> 77.4 us (0.74)
  Pallas kernels: 93.7 us -> 76.6 us
  local copies, waits for them, and re-layouts: 10.6 us -> 0 us
    pallas_call x1 -> x2, Pallas kernels: 93.7 us -> 76.6 us  [the longest x1 73.4 us: on_device(): pl.pallas_call(body, out_shape=(jax.ShapeDtypeStruct((2, 1024, HALF), bf1...]
    reshape x10 -> x0, local copies, waits for them, and re-layouts: 5.79 us -> none  [the longest x3 1.4 us: on_device(): conv_weight.reshape(10, 3, 3, 2, HALF).transpose(3, 1, 0, 2, 4)]
    slice x2 -> x0, local copies, waits for them, and re-layouts: 2.07 us -> none  [the longest x1 1.19 us: on_device(): wg[:, :, :10, :3 * HALF].reshape(2, 3, 10, 3, HALF).transpose(2, 1, 3, 0, 4)]
    another operation x2 -> x0, local copies, waits for them, and re-layouts: 1.34 us -> none  [the longest x1 0.67 us: on_device(): gb[:, 0].reshape(CH)]
    unnamed x7 -> x0, local copies, waits for them, and re-layouts: 1.07 us -> none
where the time goes in v2:
time: 77.4 us; the launch traced here: 77.2 us
  Pallas kernels  76.6 us (99%)
    pallas_call x1, Pallas kernels, on_device(): pl.pallas_call(body, out_shape=(jax.ShapeDtypeStruct((2, 1024, HALF), bf1...  73.4 us
    pallas_call x1, Pallas kernels, on_device(): pl.pallas_call(join_halves, out_shape=(jax.ShapeDtypeStruct((1024, CH), b...  3.21 us

profile of v2, /device:TPU:1, one launch (start us, length us, event | category | flops | bytes accessed | tf_op | source)
XLA Modules:
  0.0 77.2 jit_solution(14626038430020435017)
XLA Ops:
  0.6 73.4 %shard_map.102 = (bf16[2,1024,320]{2,1,0:T(8,128)(2,1)}, f32[2,3,16,1024]{3,2,1,0:T(8,128)}, f32[2,8,320]{2,1,0:T(8,128)}) custom-call(bf16[1024,640]{1,0:T(8,128)(2,1)} %bitcast.3, bf16[4,256,640]{2,1,0:T(8,128)(2,1)} %bitcast.4, bf16[10,5760]{1,0:T(8,128)(2,1)} %refs_2_.1, f32[640]{0:T(1024)} %refs_3_.1, f32[640]{0:T(1024)} %refs_4_.1, s32[80]{0:T(128)} %refs_5_.1, ...), custom_call_target="tpu_custom_call" | custom-call | tf_op jit(solution)/shard_map/pallas_call | solution.py:630
  74.0 3.2 %shard_map.103 = (bf16[1024,640]{1,0:T(8,128)(2,1)}, f32[10,5760]{1,0:T(8,128)}, f32[640]{0:T(1024)}, f32[640]{0:T(1024)}) custom-call(bf16[2,1024,320]{2,1,0:T(8,128)(2,1)} %get-tuple-element.11.ig_ref, f32[2,3,16,1024]{3,2,1,0:T(8,128)} %get-tuple-element.12.fin, f32[2,8,320]{2,1,0:T(8,128)} %get-tuple-element.13.gb_ref), custom_call_target="tpu_custom_call" | custom-call | tf_op jit(solution)/shard_map/pallas_call | solution.py:642

commit v3 on v2

--- a/solution.py
+++ b/solution.py
@@ -31,13 +31,13 @@
 def kernel(
     scale,
     x_hbm, g_hbm, w_ref, gain_ref, bias_ref, fwd_ref, bwd_ref,
-    ig_ref, fin, gb_ref,
-    wpc, x_ref, xs, xb, gp, gt, pm, ap, p1, w, y_acc, pre,
+    ig_hbm, wg_ref, gg_ref, bg_ref,
+    wpc, fin, x_ref, xs, xb, gp, gt, pm, ap, p1, w, y_acc, pre,
     cen, inv, s1, s2, m1, m2,
-    s_buf, wgs, xr, zs, zr, yf, ys, yr, ds_, dr,
-    sgp, igs, igr, hs, hr, selm, a1s, a1r, a2s, a2r,
+    s_buf, wgs, xr, z1s, z1r, z2s, z2r, yf, ys, yr, ds_, dr,
+    sgp, igs, igr, igo, hs, hr, selm, a1s, a1r, a2s, a2r,
     loc_sem, ex_s, ex_r, p1_s, p1_r, zo_s, zo_r, zf_s, zf_r, cr_s, cr_r, yi_s, yi_r,
-    x_s, x_r, z_ss, z_rs, y_ss, y_rs, d_ss, d_rs, h_ss, h_rs, a1_ss, a1_rs, a2_ss, a2_rs,
+    x_s, x_r, z1_ss, z1_rs, z2_ss, z2_rs, y_ss, y_rs, d_ss, d_rs, h_ss, h_rs, a1_ss, a1_rs, a2_ss, a2_rs,
 ):
     f = lax.axis_index("frames")
     d = lax.axis_index("dp")
@@ -88,18 +88,25 @@
         for a in range(3):
             taps = [w_ref[:, (3 * a + b) * CH + h * HALF : (3 * a + b) * CH + (h + 1) * HALF].astype(f32) for b in range(3)]
             wide.append(jnp.concatenate(taps + [jnp.zeros((10, WIDE - 3 * HALF), f32)], axis=1))
-        pieces = [wide[a][:, lb * 128 : lb * 128 + 128] for lb in range(8) for a in range(3)]
-        wpc[h] = jnp.concatenate(pieces, axis=0).astype(bf16)
+        for half in range(2):
+            pieces = [wide[a][:, lb * 128 : lb * 128 + 128] for lb in range(4 * half, 4 * half + 4) for a in range(3)]
+            wpc[h, half] = jnp.concatenate(pieces + [jnp.zeros((8, 128), f32)], axis=0).astype(bf16)
     pl.semaphore_wait(barrier, len(partners))
     me8 = (y0 * 2 + xl) * 2 + c
-    p1c = []
-    k = 0
-    for yy, xx, dc in ((y, x, 1), (y, xin, 0), (y, xin, 1), (yin, x, 0), (yin, x, 1), (yin, xin, 0), (yin, xin, 1)):
-        cc = c + dc - 2 * c * dc
-        p1c.append(remote(wpc.at[cc], p1.at[me8], p1_s.at[k], p1_r.at[k], dev(z, yy, xx, cc)))
-        k += 1
-    for cp in p1c:
-        cp.start()
+    def p1_all(half):
+        seven = p1.at[0:7, half]
+        return remote(seven, seven, p1_s.at[half], p1_r.at[half], sib)
+
+    p1c = ([], [])
+    for half in range(2):
+        k = 0
+        for yy, xx, dc in ((yin, xin, 0), (yin, xin, 1), (yin, x, 0), (yin, x, 1), (y, xin, 0), (y, xin, 1), (y, x, 1)):
+            cc = c + dc - 2 * c * dc
+            to = dev(z, yy, xx, cc)
+            p1c[half].append(remote(wpc.at[cc, half], p1.at[me8, half], p1_s.at[half], p1_r.at[half], to))
+            k += 1
+        for cp in p1c[half]:
+            cp.start()
     interior = (pl.ds(c * 4, 4), pl.ds(16, 256))
     g_local = pltpu.make_async_copy(g_hbm, gp.at[interior], loc_sem.at[0])
     g_remote = remote(g_hbm, gp.at[interior], ex_s.at[0], ex_r.at[0], sib)
@@ -163,15 +170,18 @@
 
     lax.fori_loop(0, 4, transpose_mine, 0)
 
-    for cp in p1c:
-        cp.wait_recv()
     blk = z * 2 + y1
-    oblk = 1 - 2 * y1
-    for lb in range(8):
-        for a in range(3):
-            r = (lb * 3 + a) * 10
-            piece = jnp.concatenate([p1[s, r : r + 10, :].astype(f32) for s in range(8)], axis=0)
-            w[a, blk, :, lb * 128 : lb * 128 + 128] = piece.astype(bf16)
+
+    def dense(half):
+        p1_all(half).wait_recv()
+        for lb in range(4):
+            for a in range(3):
+                r = (lb * 3 + a) * 10
+                piece = jnp.concatenate([p1[s, half, r : r + 10, :].astype(f32) for s in range(8)], axis=0)
+                at = (half * 4 + lb) * 128
+                w[a, blk, :, at : at + 128] = piece.astype(bf16)
+
+    dense(0)
 
     def lanes(qq, n=256):
         return pl.ds(pl.multiple_of(qq * 256, 256), n)
@@ -184,36 +194,41 @@
 
     def z_own(k, j):
         s = wsl(blk, quarter(j))
-        return remote(s, s, zo_s.at[k, j], zo_r.at[k, j], dev((zp, zm)[k], y, x, c))
+        return remote(s, s, zo_s.at[0], zo_r.at[j], dev((zp, zm)[k], y, x, c))
 
     def z_fwd(j):
         up = j % 2 == 0
         s = wsl((zm if up else zp) * 2 + y1, quarter(j))
-        return remote(s, s, zf_s.at[j], zf_r.at[j], dev(zp if up else zm, y, x, c))
+        return remote(s, s, zf_s.at[0], zf_r.at[j], dev(zp if up else zm, y, x, c))
 
     zrel = (z, zm, zp, zo)
 
     def cross(k, h):
         s = wsl(zrel[k] * 2 + y1, 2 * h + 1 - y0)
-        return remote(s, s, cr_s.at[k, h], cr_r.at[k, h], dev(z, ycross, x, c))
+        return remote(s, s, cr_s.at[0], cr_r.at[k, h], dev(z, ycross, x, c))
 
     def inner(k, h):
         s = wsl(zrel[k] * 2 + 1 - y1, 2 * h + y0)
-        return remote(s, s, yi_s.at[k, h], yi_r.at[k, h], dev(z, yin, x, c))
+        return remote(s, s, yi_s.at[0], yi_r.at[h], dev(z, yin, x, c))
+
+    def inner_all(h):
+        one = w.at[:, 0]
+        return remote(one, one, yi_s.at[0], yi_r.at[h], sib)
 
     def z_start(j):
         z_own(0, j).start()
         z_own(1, j).start()
 
     def z_wait(j):
-        z_own(0, j).wait_recv()
-        z_own(1, j).wait_recv()
+        two = w.at[:, 0:2, :, 0:256]
+        remote(two, two, zo_s.at[0], zo_r.at[j], sib).wait_recv()
 
     def hook_in(k, h):
         cross(k, h).wait_recv()
         inner(k, h).start()
 
     def hook0():
+        dense(1)
         z_start(1)
         cross(0, 1).start()
 
@@ -222,40 +237,40 @@
         z_fwd(0).start()
         cross(1, 0).start()
         hook_in(0, 0)
+        z_start(2)
 
     def hook2():
         cross(2, 0).start()
-        z_start(2)
 
     def hook3():
         z_wait(1)
         z_fwd(1).start()
-        cross(1, 1).start()
         hook_in(0, 1)
+        z_start(3)
 
     def hook4():
         z_fwd(0).wait_recv()
         cross(3, 0).start()
         hook_in(1, 0)
-        z_start(3)
 
     def hook5():
-        hook_in(2, 0)
-        cross(2, 1).start()
-
-    def hook6():
+        cross(1, 1).start()
         z_wait(2)
         z_fwd(2).start()
+
+    def hook6():
+        hook_in(2, 0)
         z_fwd(1).wait_recv()
-        cross(3, 1).start()
+        cross(2, 1).start()
 
     def hook7():
         hook_in(3, 0)
+        cross(3, 1).start()
+
+    def hook8():
+        hook_in(1, 1)
         z_wait(3)
         z_fwd(3).start()
-
-    def hook8():
-        hook_in(1, 1)
 
     cross(0, 0).start()
     z_start(0)
@@ -277,6 +292,7 @@
     lax.fori_loop(0, 8, stat_sq, 0)
     inv[...] = lax.rsqrt(spread_groups(s2[...]) + EPS)
 
+    hook0()
     col = lax.broadcasted_iota(jnp.int32, (256, HALF), 0) % 16
 
     def normed_of(t):
@@ -291,22 +307,24 @@
         ap[t, 16:272, :] = cat.astype(bf16)
         return 0
 
-    lax.fori_loop(0, 2, forward, 0)
-    hook0()
-    lax.fori_loop(2, 8, forward, 0)
-    hook1()
     g_remote.wait_recv()
 
-    def transpose_other(i, _):
+    def forward_pair(i, _):
         transpose(oc * 4 + i)
-        return 0
-
-    lax.fori_loop(0, 4, transpose_other, 0)
+        forward(2 * i, 0)
+        forward(2 * i + 1, 0)
+        pl.when(i == 1)(hook1)
+        return 0
+
+    lax.fori_loop(0, 4, forward_pair, 0)
     hook2()
 
     def x_copy(i, k):
         to = (xin, xcross)[k]
-        return remote(wgs.at[i, k], xr.at[i, k], x_s.at[i, k], x_r.at[i, k], dev(z, y, to, c))
+        return remote(wgs.at[i, k], xr.at[i, k], x_s.at[0], x_r.at[i], dev(z, y, to, c))
+
+    def x_all(i):
+        return remote(wgs.at[i], xr.at[i], x_s.at[0], x_r.at[i], sib)
 
     def wg_step(i, _):
         a, n = i // 2, i % 2
@@ -326,34 +344,54 @@
         pl.when(i == 4)(lambda: stage1(0))
         return 0
 
-    def z_copy(i, k):
-        return remote(zs.at[i, k], zr.at[i, k], z_ss.at[i, k], z_rs.at[i, k], dev((zp, zm, zo)[k], y, x, c))
+    def z1_copy(i, k):
+        return remote(z1s.at[i, k], z1r.at[i, k], z1_ss.at[0], z1_rs.at[i], dev((zp, zm)[k], y, x, c))
+
+    def z1_all(i):
+        return remote(z1s.at[i], z1r.at[i], z1_ss.at[0], z1_rs.at[i], sib)
+
+    def z2_copy(i, k):
+        return remote(z2s.at[i, k], z2r.at[i, k], z2_ss.at[0], z2_rs.at[i], dev((zp, zm)[k], y, x, c))
+
+    def z2_all(i):
+        return remote(z2s.at[i], z2r.at[i], z2_ss.at[0], z2_rs.at[i], sib)
 
     def y_copy(i, r):
         dy, dc = r // 2, r % 2
         yy, cc = (y + dy) % 4, c + dc - 2 * c * dc
-        return remote(ys.at[i, yy * 2 + cc], yr.at[i, r], y_ss.at[i, r], y_rs.at[i, r], dev(z, yy, x, cc))
+        return remote(ys.at[i, yy * 2 + cc], yr.at[i, r], y_ss.at[0], y_rs.at[i], dev(z, yy, x, cc))
+
+    def y_all(i):
+        seven = yr.at[i, 1:8]
+        return remote(seven, seven, y_ss.at[0], y_rs.at[i], sib)
 
     def d_copy(i):
-        return remote(ds_.at[i], dr.at[i], d_ss.at[i], d_rs.at[i], dev(z, y, xop, c))
+        return remote(ds_.at[i], dr.at[i], d_ss.at[0], d_rs.at[0], dev(z, y, xop, c))
 
     def block(b):
         return rows16(b * 80, 80)
 
     def stage1(i):
-        x_copy(i, 0).wait_recv()
-        x_copy(i, 1).wait_recv()
+        x_all(i).wait_recv()
         s_buf[i, :, :256] = s_buf[i, :, :256] + xr[i, 0].astype(f32)
         s_buf[i, :, 256:] = s_buf[i, :, 256:] + xr[i, 1].astype(f32)
-        for k in range(3):
-            zs[i, k] = s_buf[i, block((zp, zm, zo)[k]), :].astype(bf16)
-            z_copy(i, k).start()
+        z1s[i, 0] = s_buf[i, block(zo), 0:256].astype(bf16)
+        z1s[i, 1] = s_buf[i, block(zo), 256:512].astype(bf16)
+        z1_copy(i, 0).start()
+        z1_copy(i, 1).start()
+
+    def relay(i):
+        z1_all(i).wait_recv()
+        z2s[i, 0, :, 0:256] = (s_buf[i, block(zp), 0:256] + z1r[i, 0].astype(f32)).astype(bf16)
+        z2s[i, 0, :, 256:512] = s_buf[i, block(zp), 256:512].astype(bf16)
+        z2_copy(i, 0).start()
+        z2s[i, 1, :, 0:256] = s_buf[i, block(zm), 0:256].astype(bf16)
+        z2s[i, 1, :, 256:512] = (s_buf[i, block(zm), 256:512] + z1r[i, 1].astype(f32)).astype(bf16)
+        z2_copy(i, 1).start()
 
     def stage2(i):
-        total = s_buf[i, block(z), :]
-        for k in range(3):
-            z_copy(i, k).wait_recv()
-            total = total + zr[i, k].astype(f32)
+        z2_all(i).wait_recv()
+        total = s_buf[i, block(z), :] + z2r[i, 0].astype(f32) + z2r[i, 1].astype(f32)
         total = jnp.concatenate([total, jnp.zeros((8, 512), f32)], axis=0)
         for k in range(8):
             piece = total[10 * k : 10 * k + 16, :]
@@ -363,8 +401,7 @@
             y_copy(i, r).start()
 
     def stage3(i):
-        for r in range(1, 8):
-            y_copy(i, r).wait_recv()
+        y_all(i).wait_recv()
         own = yf[i, y * 2 + c]
         for dy in (1, 2, 3):
             own = own + yr[i, 2 * dy].astype(f32)
@@ -376,7 +413,6 @@
         d_copy(i).start()
 
     def stage4(i):
-        d_copy(i).wait_recv()
         own = (ds_[i, 0] + dr[i, 0]) * scale
         other = (ds_[i, 1] + dr[i, 1]) * scale
         a, n = i // 2, i % 2
@@ -386,8 +422,8 @@
 
     lax.fori_loop(0, 6, wg_step, 0)
     stage1(1)
-    for k in range(4):
-        inner(k, 0).wait_recv()
+    relay(0)
+    inner_all(0).wait_recv()
     z_fwd(2).wait_recv()
 
     def back1(t, _):
@@ -416,8 +452,9 @@
             back1(t, 0)
 
     def group_terms():
-        m1[...] = spread_groups(s2[...] * gain)
-        m2[...] = spread_groups(s1[...] * gain)
+        both = spread_groups(jnp.concatenate([s2[...] * gain, s1[...] * gain], axis=0))
+        m1[...] = both[0:8]
+        m2[...] = both[8:16]
 
     halo = [
         remote(hs.at[0], hr.at[0], h_ss.at[0], h_rs.at[0], nxt),
@@ -428,7 +465,6 @@
     selm[1] = (ch_id == fwd_ref[...].reshape(1, 80)).astype(f32).astype(bf16)
 
     def edge_frames():
-        back1_of((0, 1, 6, 7))
         group_terms()
         back2(0, 0)
         back2(7, 0)
@@ -437,17 +473,8 @@
         halo[0].start()
         halo[1].start()
 
-    def act_step(i, _):
-        n = i // 4
-        tt = (i + 3 * n) % 4
-
-        @pl.when(i == 4)
-        def _():
-            for k in range(4):
-                inner(k, 1).wait_recv()
-            z_fwd(3).wait_recv()
-
-        cols = pl.ds(pl.multiple_of(n * 512, 512), 512)
+    def act_dot(n, tt):
+        cols = pl.ds(n * 512, 512)
         lhs = jnp.concatenate(
             [
                 jnp.concatenate([gp[tt * 2 + t, 16 * (2 - a) : 16 * (2 - a) + 256, :] for a in range(3)], axis=1)
@@ -457,47 +484,70 @@
         )
         rhs = w[:, :, :, cols].reshape(3 * CH, 512)
         y_acc[rows16(tt * 512, 512), cols] = dot(lhs, rhs)
+
+    def act_step(i, _):
+        act_dot(0, i)
         plan = {
-            0: [(stage1, 2)],
-            1: [],
-            2: [(stage2, 0), (stage1, 3)],
-            3: [(stage2, 1)],
-            4: [(stage1, 4)],
-            5: [(stage3, 0), (stage2, 2), (stage1, 5)],
-            6: [(stage3, 1), (stage2, 3)],
-            7: [(stage3, 2), (stage2, 4)],
+            0: [(stage1, 2), (relay, 1)],
+            1: [(stage2, 0)],
+            2: [(stage1, 3)],
+            3: [(relay, 2), (stage2, 1)],
         }
-        for k, work in plan.items():
+        for k in range(4):
 
             @pl.when(i == k)
-            def _(k=k, work=work):
-                if k < 2:
-                    hook_in(k + 2, 1)
-                for stage, chunk in work:
+            def _(k=k):
+                if k == 0:
+                    hook_in(2, 1)
+                if k == 2:
+                    hook_in(3, 1)
+                for stage, chunk in plan.get(k, []):
                     stage(chunk)
 
-        pl.when(i == 5)(edge_frames)
-        return 0
-
-    lax.fori_loop(0, 8, act_step, 0)
+        return 0
+
+    lax.fori_loop(0, 4, act_step, 0)
+    stage1(4)
+    inner_all(1).wait_recv()
+    z_fwd(3).wait_recv()
+    act_dot(1, 3)
+    relay(3)
+    act_dot(1, 0)
+    back1_of((6, 7))
+    stage1(5)
+    relay(4)
+    stage2(2)
+    act_dot(1, 1)
+    back1_of((0, 1))
+    stage3(0)
+    edge_frames()
+    act_dot(1, 2)
+    stage2(3)
+    relay(5)
+    back1_of((2, 3))
+    stage3(1)
 
     def a1_copy(r):
         dx, dc = r // 2, r % 2
         cc = c + dc - 2 * c * dc
-        return remote(a1s, a1r.at[r], a1_ss.at[r], a1_rs.at[r], dev(z, y, (x + dx) % 4, cc))
+        return remote(a1s, a1r.at[r], a1_ss.at[0], a1_rs.at[0], dev(z, y, (x + dx) % 4, cc))
 
     def a2_copy(r):
-        return remote(a2s, a2r.at[r], a2_ss.at[r], a2_rs.at[r], dev((z + r // 4) % 4, (y + r % 4) % 4, x, c))
-
-    back1_of((2, 3, 4, 5))
+        return remote(a2s, a2r.at[r], a2_ss.at[0], a2_rs.at[0], dev((z + r // 4) % 4, (y + r % 4) % 4, x, c))
+
+    a1_all = remote(a1r.at[1:8], a1r.at[1:8], a1_ss.at[0], a1_rs.at[0], sib)
+    a2_all = remote(a2r.at[1:16], a2r.at[1:16], a2_ss.at[0], a2_rs.at[0], sib)
+
+    back1_of((4, 5))
     total = [jnp.sum(v[...], axis=0, keepdims=True) for v in (s1, s2)]
     a1s[...] = jnp.concatenate(total + [jnp.zeros((6, HALF), f32)], axis=0)
     for r in range(1, 8):
         a1_copy(r).start()
-    stage2(5)
+    stage2(4)
     group_terms()
     lax.fori_loop(1, 7, back2, 0)
-    stage3(3)
+    stage3(2)
+    stage2(5)
     halo[0].wait_recv()
     halo[1].wait_recv()
     keep_prev = jnp.where(f >= 2, 1.0, 0.0)
@@ -519,9 +569,7 @@
     lax.fori_loop(0, 4, shift_other, 0)
     i_copy = remote(igs, igr, ex_s.at[2], ex_r.at[2], sib)
     i_copy.start()
-    stage3(4)
-    for r in range(1, 8):
-        a1_copy(r).wait_recv()
+    a1_all.wait_recv()
     own = a1s[0:2, :]
     for r in (2, 4, 6):
         own = own + a1r[r, 0:2, :]
@@ -531,71 +579,65 @@
     a2s[...] = jnp.concatenate([own, other, jnp.zeros((4, HALF), f32)], axis=0)
     for r in range(1, 16):
         a2_copy(r).start()
+    stage3(3)
+    stage3(4)
     stage3(5)
-
-    def keep(i, _):
-        ig_ref[c, rows16(i * 256, 256), :] = shift(c * 4 + i).astype(bf16)
-        return 0
-
-    lax.fori_loop(0, 4, keep, 0)
     i_copy.wait_recv()
-    ig_ref[oc] = igr[...].reshape(1024, HALF)
-    for i in range(5):
-        stage4(i)
-    total = a2s[...]
-    for r in range(1, 16):
-        a2_copy(r).wait_recv()
-        total = total + a2r[r]
-    total = total * scale
-    gb_ref[c, 0:2, :] = total[0:2, :]
-    gb_ref[oc, 0:2, :] = total[2:4, :]
-    stage4(5)
-
-    for cp in p1c:
-        cp.wait_send()
+
+    def assemble(i, _):
+        own = shift(c * 4 + i)
+        other = igr[i].astype(f32)
+        v = jnp.concatenate([jnp.where(mine0, own, other), jnp.where(mine0, other, own)], axis=1)
+        igo[rows16(i * 256, 256), :] = v.astype(bf16)
+        return 0
+
+    lax.fori_loop(0, 4, assemble, 0)
+    o_copy = pltpu.make_async_copy(igo, ig_hbm, loc_sem.at[2])
+    o_copy.start()
+
+    p1_all(0).wait_send()
+    p1_all(1).wait_send()
     for cp in (g_remote, x_remote, i_copy, halo[0], halo[1]):
         cp.wait_send()
-    for qq in range(4):
-        z_own(0, qq).wait_send()
-        z_own(1, qq).wait_send()
-        z_fwd(qq).wait_send()
-    for k in range(4):
-        for h in range(2):
-            cross(k, h).wait_send()
-            inner(k, h).wait_send()
-    for r in range(1, 8):
-        a1_copy(r).wait_send()
-    for r in range(1, 16):
-        a2_copy(r).wait_send()
-
-    def drain(i, _):
-        for k in range(2):
-            x_copy(i, k).wait_send()
-        for k in range(3):
-            z_copy(i, k).wait_send()
-        for r in range(1, 8):
-            y_copy(i, r).wait_send()
-        d_copy(i).wait_send()
-        return 0
-
-    lax.fori_loop(0, 6, drain, 0)
-
-
-def join_halves(ig_ref, fin, gb_ref, out_ref, wg_ref, gg_ref, bg_ref):
-    def rows(i, _):
-        r = rows16(i * 256, 256)
-        both = jnp.concatenate([ig_ref[0, r, :].astype(f32), ig_ref[1, r, :].astype(f32)], axis=1)
-        out_ref[r, :] = both.astype(bf16)
-        return 0
-
-    lax.fori_loop(0, 4, rows, 0)
+    one, two = w.at[:, 0], w.at[:, 0:2]
+    for ref, sem in ((two, zo_s), (one, zf_s), (two, cr_s), (two, yi_s), (wgs, x_s), (z1s, z1_ss), (z2s, z2_ss), (yr.at[:, 1:8], y_ss)):
+        remote(ref, ref, sem.at[0], sem.at[0], sib).wait_send()
+    a1_all.wait_send()
+
+    remote(ds_, dr, d_ss.at[0], d_rs.at[0], sib).wait_recv()
+    for i in range(6):
+        stage4(i)
     for a in range(3):
         for b in range(3):
             tap = jnp.concatenate([fin[h, a, 0:10, b * HALF : (b + 1) * HALF] for h in range(2)], axis=1)
             wg_ref[:, (3 * a + b) * CH : (3 * a + b + 1) * CH] = tap
-    both = jnp.concatenate([gb_ref[0, 0:2, :], gb_ref[1, 0:2, :]], axis=1)
+    total = a2s[...]
+    a2_all.wait_recv()
+    for r in range(1, 16):
+        total = total + a2r[r]
+    total = total * scale
+    own, other = total[0:2, :], total[2:4, :]
+    both = jnp.concatenate([jnp.where(mine0, own, other), jnp.where(mine0, other, own)], axis=1)
     gg_ref[...] = both[0:1, :].reshape(CH)
     bg_ref[...] = both[1:2, :].reshape(CH)
+    a2_all.wait_send()
+    remote(ds_, dr, d_ss.at[0], d_rs.at[0], sib).wait_send()
+    o_copy.wait()
+
+
+def hand_over(ig_in, wg_in, gg_in, bg_in, ig_out, wg_out, gg_out, bg_out, ig, wg, gg, bg, in_sem, out_sem):
+    rows = [pl.ds(256 * k, 256) for k in range(4)]
+    sets = [(ig_in.at[r], ig.at[r], ig_out.at[r]) for r in rows]
+    sets += [(wg_in, wg, wg_out), (gg_in, gg, gg_out), (bg_in, bg, bg_out)]
+    first = [pltpu.make_async_copy(a, b, in_sem.at[k]) for k, (a, b, _) in enumerate(sets)]
+    second = [pltpu.make_async_copy(b, d, out_sem.at[k]) for k, (_, b, d) in enumerate(sets)]
+    for cp in first:
+        cp.start()
+    for a, b in zip(first, second):
+        a.wait()
+        b.start()
+    for cp in second:
+        cp.wait()
 
 
 def on_device(shifted, out_grad, conv_weight, norm_gain, norm_bias, shift_fwd, shift_bwd):
@@ -605,50 +647,51 @@
     dma = pltpu.SemaphoreType.DMA
     vm = pltpu.VMEM
     scratch = [
-        vm((2, 240, 128), bf16), vm((1024, CH), bf16),
+        vm((2, 2, 128, 128), bf16), vm((2, 3, 16, WIDE), f32), vm((1024, CH), bf16),
         vm((2, 1024, HALF), bf16), vm((1024, HALF), bf16), vm((8, 288, CH), bf16), vm((CH, 2048), bf16),
-        vm((CH, CH), bf16), vm((8, 288, WIDE), bf16), vm((8, 240, 128), bf16), vm((3, 8, 80, WIDE), bf16),
+        vm((CH, CH), bf16), vm((8, 288, WIDE), bf16), vm((8, 2, 128, 128), bf16), vm((3, 8, 80, WIDE), bf16),
         vm((2048, WIDE), f32), vm((2048, HALF), f32),
         vm((8, HALF), f32), vm((8, HALF), f32), vm((8, HALF), f32), vm((8, HALF), f32), vm((8, HALF), f32), vm((8, HALF), f32),
         vm((6, HALF, 512), f32), vm((6, 2, HALF, 256), bf16), vm((6, 2, HALF, 256), bf16),
-        vm((6, 3, 80, 512), bf16), vm((6, 3, 80, 512), bf16),
+        vm((6, 2, 80, 256), bf16), vm((6, 2, 80, 256), bf16), vm((6, 2, 80, 512), bf16), vm((6, 2, 80, 512), bf16),
         vm((6, 8, 16, 512), f32), vm((6, 8, 16, 512), bf16), vm((6, 8, 16, 512), bf16),
         vm((6, 2, 16, 512), f32), vm((6, 2, 16, 512), f32),
-        vm((10, 256, HALF), bf16), vm((4, 256, HALF), bf16), vm((4, 256, HALF), bf16),
+        vm((10, 256, HALF), bf16), vm((4, 256, HALF), bf16), vm((4, 256, HALF), bf16), vm((1024, CH), bf16),
         vm((2, 256, 80), bf16), vm((2, 256, 80), bf16), vm((2, HALF, 80), bf16),
         vm((8, HALF), f32), vm((8, 8, HALF), f32), vm((8, HALF), f32), vm((16, 8, HALF), f32),
-        dma((2,)), dma((4,)), dma((4,)), dma((7,)), dma((7,)), dma((2, 4)), dma((2, 4)), dma((4,)), dma((4,)),
-        dma((4, 2)), dma((4, 2)), dma((4, 2)), dma((4, 2)),
-        dma((6, 2)), dma((6, 2)), dma((6, 3)), dma((6, 3)), dma((6, 8)), dma((6, 8)),
-        dma((6,)), dma((6,)), dma((2,)), dma((2,)), dma((8,)), dma((8,)), dma((16,)), dma((16,)),
+        dma((4,)), dma((4,)), dma((4,)), dma((2,)), dma((2,)), dma((1,)), dma((4,)), dma((1,)), dma((4,)),
+        dma((1,)), dma((4, 2)), dma((1,)), dma((2,)),
+        dma((1,)), dma((6,)), dma((1,)), dma((6,)), dma((1,)), dma((6,)), dma((1,)), dma((6,)),
+        dma((1,)), dma((1,)), dma((2,)), dma((2,)), dma((1,)), dma((1,)), dma((1,)), dma((1,)),
     ]
     v = pl.BlockSpec(memory_space=pltpu.VMEM)
 
     def body(*refs):
         kernel(scale, *refs)
 
+    shapes = (
+        jax.ShapeDtypeStruct((1024, CH), bf16),
+        jax.ShapeDtypeStruct((10, 9 * CH), f32),
+        jax.ShapeDtypeStruct((CH,), f32),
+        jax.ShapeDtypeStruct((CH,), f32),
+    )
+    anywhere = pl.BlockSpec(memory_space=pl.ANY)
     parts = pl.pallas_call(
         body,
-        out_shape=(
-            jax.ShapeDtypeStruct((2, 1024, HALF), bf16),
-            jax.ShapeDtypeStruct((2, 3, 16, WIDE), f32),
-            jax.ShapeDtypeStruct((2, 8, HALF), f32),
-        ),
+        out_shape=shapes,
         in_specs=[pl.BlockSpec(memory_space=pl.ANY), pl.BlockSpec(memory_space=pl.ANY), v, v, v, v, v],
-        out_specs=(v, v, v),
+        out_specs=(anywhere, v, v, v),
         scratch_shapes=scratch,
         compiler_params=pltpu.CompilerParams(collective_id=0, has_side_effects=True, vmem_limit_bytes=60 << 20),
     )(x, g, conv_weight, norm_gain, norm_bias, shift_fwd, shift_bwd)
     ig, wg, gg, bg = pl.pallas_call(
-        join_halves,
-        out_shape=(
-            jax.ShapeDtypeStruct((1024, CH), bf16),
-            jax.ShapeDtypeStruct((10, 9 * CH), f32),
-            jax.ShapeDtypeStruct((CH,), f32),
-            jax.ShapeDtypeStruct((CH,), f32),
-        ),
-        in_specs=[v, v, v],
-        out_specs=(v, v, v, v),
+        hand_over,
+        out_shape=shapes,
+        in_specs=[anywhere] * 4,
+        out_specs=(anywhere,) * 4,
+        scratch_shapes=[
+            vm((1024, CH), bf16), vm((10, 9 * CH), f32), vm((CH,), f32), vm((CH,), f32), dma((7,)), dma((7,)),
+        ],
     )(*parts)
     return (ig.reshape(shifted.shape), wg, gg, bg)
 

time: 77.4 us -> 72.6 us (0.938)
  Pallas kernels: 76.6 us -> 71.8 us
    pallas_call x2, Pallas kernels: 76.6 us -> 71.8 us  [the longest x1 69.5 us: on_device(): pl.pallas_call(body, out_shape=shapes, in_specs=[pl.BlockSpec(memory_spac...]
where the time goes in v3:
time: 72.6 us; the launch traced here: 72.4 us
  Pallas kernels  71.8 us (99%)
    pallas_call x1, Pallas kernels, on_device(): pl.pallas_call(body, out_shape=shapes, in_specs=[pl.BlockSpec(memory_spac...  69.5 us
    pallas_call x1, Pallas kernels, on_device(): pl.pallas_call(hand_over, out_shape=shapes, in_specs=[anywhere] * 4, out_...  2.27 us

profile of v3, /device:TPU:1, one launch (start us, length us, event | category | flops | bytes accessed | tf_op | source)
XLA Modules:
  0.0 72.4 jit_solution(15327495287577265881)
XLA Ops:
  0.6 69.5 %shard_map.102 = (bf16[1024,640]{1,0:T(8,128)(2,1)}, f32[10,5760]{1,0:T(8,128)}, f32[640]{0:T(1024)}, f32[640]{0:T(1024)}) custom-call(bf16[1024,640]{1,0:T(8,128)(2,1)} %bitcast.3, bf16[4,256,640]{2,1,0:T(8,128)(2,1)} %bitcast.4, bf16[10,5760]{1,0:T(8,128)(2,1)} %refs_2_.1, f32[640]{0:T(1024)} %refs_3_.1, f32[640]{0:T(1024)} %refs_4_.1, s32[80]{0:T(128)} %refs_5_.1, ...), custom_call_target="tpu_custom_call" | custom-call | tf_op jit(solution)/shard_map/pallas_call | solution.py:679
  70.2 2.3 %shard_map.103 = (bf16[1024,640]{1,0:T(8,128)(2,1)}, f32[10,5760]{1,0:T(8,128)}, f32[640]{0:T(1024)}, f32[640]{0:T(1024)}) custom-call(bf16[1024,640]{1,0:T(8,128)(2,1)} %get-tuple-element.12.ig_in, f32[10,5760]{1,0:T(8,128)} %get-tuple-element.13.wg_in, f32[640]{0:T(1024)} %get-tuple-element.14.gg_in, f32[640]{0:T(1024)} %get-tuple-element.15.bg_in), custom_call_target="tpu_custom_call" | custom-call | tf_op jit(solution)/shard_map/pallas_call | solution.py:687

commit v4 on v3

--- a/solution.py
+++ b/solution.py
@@ -9,6 +9,7 @@
 MESH = pl.DeviceIdType.MESH
 EPS = 1e-05
 CH, HALF, WIDE = 640, 320, 1024
+FULL = 384
 HIGH = lax.Precision.HIGHEST
 
 
@@ -105,8 +106,8 @@
             to = dev(z, yy, xx, cc)
             p1c[half].append(remote(wpc.at[cc, half], p1.at[me8, half], p1_s.at[half], p1_r.at[half], to))
             k += 1
-        for cp in p1c[half]:
-            cp.start()
+    for cp in p1c[0]:
+        cp.start()
     interior = (pl.ds(c * 4, 4), pl.ds(16, 256))
     g_local = pltpu.make_async_copy(g_hbm, gp.at[interior], loc_sem.at[0])
     g_remote = remote(g_hbm, gp.at[interior], ex_s.at[0], ex_r.at[0], sib)
@@ -117,8 +118,8 @@
     def split(t, _):
         r = rows16(t * 256, 256)
         v = x_ref[r, :].astype(f32)
-        xs[0, r, :] = v[:, :HALF].astype(bf16)
-        xs[1, r, :] = v[:, HALF:].astype(bf16)
+        xs[0, r, :HALF] = v[:, :HALF].astype(bf16)
+        xs[1, r, :HALF] = v[:, HALF:].astype(bf16)
         return 0
 
     lax.fori_loop(0, 4, split, 0)
@@ -128,8 +129,8 @@
 
     def read_x(t):
         r = rows16((t % 4) * 256, 256)
-        mine = xs[c, r, :]
-        other = xb[r, :]
+        mine = xs[c, r, :HALF]
+        other = xb[r, :HALF]
         return jnp.where(t // 4 == c, mine, other).astype(f32)
 
     zero16 = jnp.zeros((16, CH), bf16)
@@ -169,6 +170,25 @@
         return 0
 
     lax.fori_loop(0, 4, transpose_mine, 0)
+    for cp in p1c[1]:
+        cp.start()
+
+    x_remote.wait_recv()
+
+    def stat_sum(t, _):
+        s1[pl.ds(t, 1), :] = jnp.sum(read_x(t), axis=0, keepdims=True)
+        return 0
+
+    lax.fori_loop(0, 8, stat_sum, 0)
+    cen[...] = spread_groups(s1[...])
+
+    def stat_sq(t, _):
+        v = read_x(t) - cen[pl.ds(t, 1), :]
+        s2[pl.ds(t, 1), :] = jnp.sum(v * v, axis=0, keepdims=True)
+        return 0
+
+    lax.fori_loop(0, 8, stat_sq, 0)
+    inv[...] = lax.rsqrt(spread_groups(s2[...]) + EPS)
 
     blk = z * 2 + y1
 
@@ -275,24 +295,6 @@
     cross(0, 0).start()
     z_start(0)
 
-    x_remote.wait_recv()
-
-    def stat_sum(t, _):
-        s1[pl.ds(t, 1), :] = jnp.sum(read_x(t), axis=0, keepdims=True)
-        return 0
-
-    lax.fori_loop(0, 8, stat_sum, 0)
-    cen[...] = spread_groups(s1[...])
-
-    def stat_sq(t, _):
-        v = read_x(t) - cen[pl.ds(t, 1), :]
-        s2[pl.ds(t, 1), :] = jnp.sum(v * v, axis=0, keepdims=True)
-        return 0
-
-    lax.fori_loop(0, 8, stat_sq, 0)
-    inv[...] = lax.rsqrt(spread_groups(s2[...]) + EPS)
-
-    hook0()
     col = lax.broadcasted_iota(jnp.int32, (256, HALF), 0) % 16
 
     def normed_of(t):
@@ -313,11 +315,11 @@
         transpose(oc * 4 + i)
         forward(2 * i, 0)
         forward(2 * i + 1, 0)
-        pl.when(i == 1)(hook1)
+        pl.when(i == 1)(hook0)
         return 0
 
     lax.fori_loop(0, 4, forward_pair, 0)
-    hook2()
+    hook1()
 
     def x_copy(i, k):
         to = (xin, xcross)[k]
@@ -339,7 +341,7 @@
         x_copy(i, 0).start()
         x_copy(i, 1).start()
 
-        for k, hook in enumerate((hook3, hook4, hook5, hook6, hook7, hook8)):
+        for k, hook in enumerate((hook2, hook3, hook4, hook5, hook6, hook7)):
             pl.when(i == k)(hook)
         pl.when(i == 4)(lambda: stage1(0))
         return 0
@@ -422,6 +424,7 @@
 
     lax.fori_loop(0, 6, wg_step, 0)
     stage1(1)
+    hook8()
     relay(0)
     inner_all(0).wait_recv()
     z_fwd(2).wait_recv()
@@ -468,8 +471,8 @@
         group_terms()
         back2(0, 0)
         back2(7, 0)
-        hs[0] = dot(sgp[8], selm[0]).astype(bf16)
-        hs[1] = dot(sgp[1], selm[1]).astype(bf16)
+        hs[0, :, :80] = dot(sgp[8], selm[0]).astype(bf16)
+        hs[1, :, :80] = dot(sgp[1], selm[1]).astype(bf16)
         halo[0].start()
         halo[1].start()
 
@@ -511,19 +514,19 @@
     inner_all(1).wait_recv()
     z_fwd(3).wait_recv()
     act_dot(1, 3)
+    stage1(5)
     relay(3)
     act_dot(1, 0)
     back1_of((6, 7))
-    stage1(5)
     relay(4)
     stage2(2)
     act_dot(1, 1)
     back1_of((0, 1))
     stage3(0)
     edge_frames()
+    relay(5)
     act_dot(1, 2)
     stage2(3)
-    relay(5)
     back1_of((2, 3))
     stage3(1)
 
@@ -540,53 +543,61 @@
 
     back1_of((4, 5))
     total = [jnp.sum(v[...], axis=0, keepdims=True) for v in (s1, s2)]
-    a1s[...] = jnp.concatenate(total + [jnp.zeros((6, HALF), f32)], axis=0)
+    a1s[:, :HALF] = jnp.concatenate(total + [jnp.zeros((6, HALF), f32)], axis=0)
     for r in range(1, 8):
         a1_copy(r).start()
     stage2(4)
     group_terms()
     lax.fori_loop(1, 7, back2, 0)
+    ones = jnp.ones((8, 80), bf16)
+    bwd_mask = dot_nt(ones, selm[0])[0:1, :] > 0.5
+    fwd_mask = dot_nt(ones, selm[1])[0:1, :] > 0.5
+
+    def shift(t):
+        v = jnp.where(bwd_mask, sgp[t].astype(f32), sgp[t + 1].astype(f32))
+        return jnp.where(fwd_mask, sgp[t + 2].astype(f32), v)
+
+    def shift_other(i, _):
+        igs[i, :, :HALF] = shift(oc * 4 + i).astype(bf16)
+        return 0
+
+    lax.fori_loop(c, c + 3, shift_other, 0)
+    inside = pl.ds(c, 3)
+    i_copies = [
+        remote(igs.at[inside], igr.at[inside], ex_s.at[2], ex_r.at[2], sib),
+        remote(igs.at[3 * oc], igr.at[3 * oc], ex_s.at[3], ex_r.at[3], sib),
+    ]
+    i_copies[0].start()
     stage3(2)
     stage2(5)
     halo[0].wait_recv()
     halo[1].wait_recv()
     keep_prev = jnp.where(f >= 2, 1.0, 0.0)
     keep_next = jnp.where(f < 62, 1.0, 0.0)
-    sgp[0] = (dot_nt(hr[0], selm[0]) * keep_prev).astype(bf16)
-    sgp[9] = (dot_nt(hr[1], selm[1]) * keep_next).astype(bf16)
-    ones = jnp.ones((8, 80), bf16)
-    bwd_mask = dot_nt(ones, selm[0])[0:1, :] > 0.5
-    fwd_mask = dot_nt(ones, selm[1])[0:1, :] > 0.5
-
-    def shift(t):
-        v = jnp.where(bwd_mask, sgp[t].astype(f32), sgp[t + 1].astype(f32))
-        return jnp.where(fwd_mask, sgp[t + 2].astype(f32), v)
-
-    def shift_other(i, _):
-        igs[i] = shift(oc * 4 + i).astype(bf16)
-        return 0
-
-    lax.fori_loop(0, 4, shift_other, 0)
-    i_copy = remote(igs, igr, ex_s.at[2], ex_r.at[2], sib)
-    i_copy.start()
+    sgp[0] = (dot_nt(hr[0, :, :80], selm[0]) * keep_prev).astype(bf16)
+    sgp[9] = (dot_nt(hr[1, :, :80], selm[1]) * keep_next).astype(bf16)
+    shift_other(3 * oc, 0)
+    i_copies[1].start()
     a1_all.wait_recv()
-    own = a1s[0:2, :]
+    own = a1s[0:2, :HALF]
     for r in (2, 4, 6):
-        own = own + a1r[r, 0:2, :]
-    other = a1r[1, 0:2, :]
+        own = own + a1r[r, 0:2, :HALF]
+    other = a1r[1, 0:2, :HALF]
     for r in (3, 5, 7):
-        other = other + a1r[r, 0:2, :]
-    a2s[...] = jnp.concatenate([own, other, jnp.zeros((4, HALF), f32)], axis=0)
+        other = other + a1r[r, 0:2, :HALF]
+    a2s[:, :HALF] = jnp.concatenate([own, other, jnp.zeros((4, HALF), f32)], axis=0)
     for r in range(1, 16):
         a2_copy(r).start()
     stage3(3)
     stage3(4)
     stage3(5)
-    i_copy.wait_recv()
+    inner_frames = igr.at[0:3]
+    remote(inner_frames, inner_frames, ex_s.at[2], ex_r.at[2], sib).wait_recv()
+    i_copies[1].wait_recv()
 
     def assemble(i, _):
         own = shift(c * 4 + i)
-        other = igr[i].astype(f32)
+        other = igr[i, :, :HALF].astype(f32)
         v = jnp.concatenate([jnp.where(mine0, own, other), jnp.where(mine0, other, own)], axis=1)
         igo[rows16(i * 256, 256), :] = v.astype(bf16)
         return 0
@@ -597,7 +608,7 @@
 
     p1_all(0).wait_send()
     p1_all(1).wait_send()
-    for cp in (g_remote, x_remote, i_copy, halo[0], halo[1]):
+    for cp in (g_remote, x_remote, *i_copies, halo[0], halo[1]):
         cp.wait_send()
     one, two = w.at[:, 0], w.at[:, 0:2]
     for ref, sem in ((two, zo_s), (one, zf_s), (two, cr_s), (two, yi_s), (wgs, x_s), (z1s, z1_ss), (z2s, z2_ss), (yr.at[:, 1:8], y_ss)):
@@ -611,10 +622,10 @@
         for b in range(3):
             tap = jnp.concatenate([fin[h, a, 0:10, b * HALF : (b + 1) * HALF] for h in range(2)], axis=1)
             wg_ref[:, (3 * a + b) * CH : (3 * a + b + 1) * CH] = tap
-    total = a2s[...]
+    total = a2s[:, :HALF]
     a2_all.wait_recv()
     for r in range(1, 16):
-        total = total + a2r[r]
+        total = total + a2r[r, :, :HALF]
     total = total * scale
     own, other = total[0:2, :], total[2:4, :]
     both = jnp.concatenate([jnp.where(mine0, own, other), jnp.where(mine0, other, own)], axis=1)
@@ -648,7 +659,7 @@
     vm = pltpu.VMEM
     scratch = [
         vm((2, 2, 128, 128), bf16), vm((2, 3, 16, WIDE), f32), vm((1024, CH), bf16),
-        vm((2, 1024, HALF), bf16), vm((1024, HALF), bf16), vm((8, 288, CH), bf16), vm((CH, 2048), bf16),
+        vm((2, 1024, FULL), bf16), vm((1024, FULL), bf16), vm((8, 288, CH), bf16), vm((CH, 2048), bf16),
         vm((CH, CH), bf16), vm((8, 288, WIDE), bf16), vm((8, 2, 128, 128), bf16), vm((3, 8, 80, WIDE), bf16),
         vm((2048, WIDE), f32), vm((2048, HALF), f32),
         vm((8, HALF), f32), vm((8, HALF), f32), vm((8, HALF), f32), vm((8, HALF), f32), vm((8, HALF), f32), vm((8, HALF), f32),
@@ -656,9 +667,9 @@
         vm((6, 2, 80, 256), bf16), vm((6, 2, 80, 256), bf16), vm((6, 2, 80, 512), bf16), vm((6, 2, 80, 512), bf16),
         vm((6, 8, 16, 512), f32), vm((6, 8, 16, 512), bf16), vm((6, 8, 16, 512), bf16),
         vm((6, 2, 16, 512), f32), vm((6, 2, 16, 512), f32),
-        vm((10, 256, HALF), bf16), vm((4, 256, HALF), bf16), vm((4, 256, HALF), bf16), vm((1024, CH), bf16),
-        vm((2, 256, 80), bf16), vm((2, 256, 80), bf16), vm((2, HALF, 80), bf16),
-        vm((8, HALF), f32), vm((8, 8, HALF), f32), vm((8, HALF), f32), vm((16, 8, HALF), f32),
+        vm((10, 256, HALF), bf16), vm((4, 256, FULL), bf16), vm((4, 256, FULL), bf16), vm((1024, CH), bf16),
+        vm((2, 256, 128), bf16), vm((2, 256, 128), bf16), vm((2, HALF, 80), bf16),
+        vm((8, FULL), f32), vm((8, 8, FULL), f32), vm((8, FULL), f32), vm((16, 8, FULL), f32),
         dma((4,)), dma((4,)), dma((4,)), dma((2,)), dma((2,)), dma((1,)), dma((4,)), dma((1,)), dma((4,)),
         dma((1,)), dma((4, 2)), dma((1,)), dma((2,)),
         dma((1,)), dma((6,)), dma((1,)), dma((6,)), dma((1,)), dma((6,)), dma((1,)), dma((6,)),

time: 72.6 us -> 72 us (level)
  no operation moved by 1% of the time
where the time goes in v4:
time: 72 us; the launch traced here: 71.8 us
  Pallas kernels  71.1 us (99%)
    pallas_call x1, Pallas kernels, on_device(): pl.pallas_call(body, out_shape=shapes, in_specs=[pl.BlockSpec(memory_spac...  68.9 us
    pallas_call x1, Pallas kernels, on_device(): pl.pallas_call(hand_over, out_shape=shapes, in_specs=[anywhere] * 4, out_...  2.27 us

profile of v4, /device:TPU:1, one launch (start us, length us, event | category | flops | bytes accessed | tf_op | source)
XLA Modules:
  0.0 71.8 jit_solution(6172859942742982120)
XLA Ops:
  0.6 68.9 %shard_map.102 = (bf16[1024,640]{1,0:T(8,128)(2,1)}, f32[10,5760]{1,0:T(8,128)}, f32[640]{0:T(1024)}, f32[640]{0:T(1024)}) custom-call(bf16[1024,640]{1,0:T(8,128)(2,1)} %bitcast.3, bf16[4,256,640]{2,1,0:T(8,128)(2,1)} %bitcast.4, bf16[10,5760]{1,0:T(8,128)(2,1)} %refs_2_.1, f32[640]{0:T(1024)} %refs_3_.1, f32[640]{0:T(1024)} %refs_4_.1, s32[80]{0:T(128)} %refs_5_.1, ...), custom_call_target="tpu_custom_call" | custom-call | tf_op jit(solution)/shard_map/pallas_call | solution.py:690
  69.5 2.3 %shard_map.103 = (bf16[1024,640]{1,0:T(8,128)(2,1)}, f32[10,5760]{1,0:T(8,128)}, f32[640]{0:T(1024)}, f32[640]{0:T(1024)}) custom-call(bf16[1024,640]{1,0:T(8,128)(2,1)} %get-tuple-element.12.ig_in, f32[10,5760]{1,0:T(8,128)} %get-tuple-element.13.wg_in, f32[640]{0:T(1024)} %get-tuple-element.14.gg_in, f32[640]{0:T(1024)} %get-tuple-element.15.bg_in), custom_call_target="tpu_custom_call" | custom-call | tf_op jit(solution)/shard_map/pallas_call | solution.py:698

commit v5 on v4

--- a/solution.py
+++ b/solution.py
@@ -502,10 +502,10 @@
             def _(k=k):
                 if k == 0:
                     hook_in(2, 1)
-                if k == 2:
-                    hook_in(3, 1)
                 for stage, chunk in plan.get(k, []):
                     stage(chunk)
+                if k == 1:
+                    hook_in(3, 1)
 
         return 0
 

time: 72 us -> 71.3 us (level)
  no operation moved by 1% of the time
where the time goes in v5:
time: 71.3 us; the launch traced here: 71.1 us
  Pallas kernels  70.5 us (99%)
    pallas_call x1, Pallas kernels, on_device(): pl.pallas_call(body, out_shape=shapes, in_specs=[pl.BlockSpec(memory_spac...  68.2 us
    pallas_call x1, Pallas kernels, on_device(): pl.pallas_call(hand_over, out_shape=shapes, in_specs=[anywhere] * 4, out_...  2.27 us

profile of v5, /device:TPU:1, one launch (start us, length us, event | category | flops | bytes accessed | tf_op | source)
XLA Modules:
  0.0 71.1 jit_solution(11911274537811936513)
XLA Ops:
  0.6 68.2 %shard_map.102 = (bf16[1024,640]{1,0:T(8,128)(2,1)}, f32[10,5760]{1,0:T(8,128)}, f32[640]{0:T(1024)}, f32[640]{0:T(1024)}) custom-call(bf16[1024,640]{1,0:T(8,128)(2,1)} %bitcast.3, bf16[4,256,640]{2,1,0:T(8,128)(2,1)} %bitcast.4, bf16[10,5760]{1,0:T(8,128)(2,1)} %refs_2_.1, f32[640]{0:T(1024)} %refs_3_.1, f32[640]{0:T(1024)} %refs_4_.1, s32[80]{0:T(128)} %refs_5_.1, ...), custom_call_target="tpu_custom_call" | custom-call | tf_op jit(solution)/shard_map/pallas_call | solution.py:690
  68.8 2.3 %shard_map.103 = (bf16[1024,640]{1,0:T(8,128)(2,1)}, f32[10,5760]{1,0:T(8,128)}, f32[640]{0:T(1024)}, f32[640]{0:T(1024)}) custom-call(bf16[1024,640]{1,0:T(8,128)(2,1)} %get-tuple-element.12.ig_in, f32[10,5760]{1,0:T(8,128)} %get-tuple-element.13.wg_in, f32[640]{0:T(1024)} %get-tuple-element.14.gg_in, f32[640]{0:T(1024)} %get-tuple-element.15.bg_in), custom_call_target="tpu_custom_call" | custom-call | tf_op jit(solution)/shard_map/pallas_call | solution.py:698

commit v6 on v5

--- a/solution.py
+++ b/solution.py
@@ -424,8 +424,8 @@
 
     lax.fori_loop(0, 6, wg_step, 0)
     stage1(1)
+    relay(0)
     hook8()
-    relay(0)
     inner_all(0).wait_recv()
     z_fwd(2).wait_recv()
 
@@ -568,8 +568,8 @@
         remote(igs.at[3 * oc], igr.at[3 * oc], ex_s.at[3], ex_r.at[3], sib),
     ]
     i_copies[0].start()
+    stage2(5)
     stage3(2)
-    stage2(5)
     halo[0].wait_recv()
     halo[1].wait_recv()
     keep_prev = jnp.where(f >= 2, 1.0, 0.0)

time: 71.3 us -> 71.6 us (level)
  no operation moved by 1% of the time
where the time goes in v6:
time: 71.6 us; the launch traced here: 71.4 us
  Pallas kernels  70.7 us (99%)
    pallas_call x1, Pallas kernels, on_device(): pl.pallas_call(body, out_shape=shapes, in_specs=[pl.BlockSpec(memory_spac...  68.5 us
    pallas_call x1, Pallas kernels, on_device(): pl.pallas_call(hand_over, out_shape=shapes, in_specs=[anywhere] * 4, out_...  2.27 us

profile of v6, /device:TPU:1, one launch (start us, length us, event | category | flops | bytes accessed | tf_op | source)
XLA Modules:
  0.0 71.4 jit_solution(15410257722125367443)
XLA Ops:
  0.6 68.5 %shard_map.102 = (bf16[1024,640]{1,0:T(8,128)(2,1)}, f32[10,5760]{1,0:T(8,128)}, f32[640]{0:T(1024)}, f32[640]{0:T(1024)}) custom-call(bf16[1024,640]{1,0:T(8,128)(2,1)} %bitcast.3, bf16[4,256,640]{2,1,0:T(8,128)(2,1)} %bitcast.4, bf16[10,5760]{1,0:T(8,128)(2,1)} %refs_2_.1, f32[640]{0:T(1024)} %refs_3_.1, f32[640]{0:T(1024)} %refs_4_.1, s32[80]{0:T(128)} %refs_5_.1, ...), custom_call_target="tpu_custom_call" | custom-call | tf_op jit(solution)/shard_map/pallas_call | solution.py:690
  69.1 2.3 %shard_map.103 = (bf16[1024,640]{1,0:T(8,128)(2,1)}, f32[10,5760]{1,0:T(8,128)}, f32[640]{0:T(1024)}, f32[640]{0:T(1024)}) custom-call(bf16[1024,640]{1,0:T(8,128)(2,1)} %get-tuple-element.12.ig_in, f32[10,5760]{1,0:T(8,128)} %get-tuple-element.13.wg_in, f32[640]{0:T(1024)} %get-tuple-element.14.gg_in, f32[640]{0:T(1024)} %get-tuple-element.15.bg_in), custom_call_target="tpu_custom_call" | custom-call | tf_op jit(solution)/shard_map/pallas_call | solution.py:698
